TPU v7x, 128 devices: a whole 4x4x4 slice. The times are simulated.
128 devices in a mesh: sample: 16 (over z_lo, y, core), head: 8 (over x, z_hi).
Axes of the slice: x: 4, y: 4, z: 4 (z_hi: 2, z_lo: 2; z = z_hi * 2 + z_lo), core: 2. Of those that a mesh axis runs over, the one named last changes fastest.
Arguments:
- queries: bfloat16 [16, 512, 8192], P('sample', None, 'head'), may hold values from -12 to 12
- suffix_keys: bfloat16 [16, 512, 1024], P('sample', None, 'head'), may hold values from -4 to 4
- suffix_values: bfloat16 [16, 512, 1024], P('sample', None, 'head'), may hold values from -16 to 16
- prefix_keys: bfloat16 [4096, 1024], P('sample', 'head'), may hold values from -6 to 6
- prefix_values: bfloat16 [4096, 1024], P('sample', 'head'), may hold values from -16 to 16
- lengths: int32 [16], replicated, may hold values from 1 to 512, as said below
- out_weight: bfloat16 [8192, 5120], P('head', 'sample'), may hold values from -0.0625 to 0.0625
Outputs:
- projected: bfloat16 [16, 512, 5120], P('sample', 'head')
Inputs may be any that keep to these rules, and one draw needn't show every extreme that they name: `lengths`: some sample's length is exactly 512.
All inputs are finite; a program needn't handle non-finite values.
Results may differ from a plain program's by a relative error of at most 0.018.
Values may be sent and summed in bfloat16 or wider, within the bound.
No kernel may reach another device: no remote copies, remote signals or barrier semaphores. Data moves between devices by JAX's collectives and lax.ppermute only.
A program may use at most 128 MiB of HBM per device.

v0:
```python
import jax
import jax.numpy as jnp
from jax import lax
from jax.sharding import PartitionSpec as P

HQ = 64
KVH = 8
HD = 128
BLK = 64


def update(state_now, query_block, key_rows, value_rows, visible):
    row_maxes, totals, accumulated = state_now
    kv_heads = key_rows.shape[1] // HD
    grouped = query_block.reshape(query_block.shape[0], kv_heads, HQ // KVH, HD)
    keyed_rows = key_rows.reshape(key_rows.shape[0], kv_heads, HD)
    valued_rows = value_rows.reshape(value_rows.shape[0], kv_heads, HD)
    scores = jnp.einsum(
        "qhgd,khd->hgqk", grouped, keyed_rows, preferred_element_type=jnp.float32
    ) * HD ** (-0.5)
    if visible is not None:
        scores = jnp.where(visible, scores, -jnp.inf)
    new_maxes = jnp.maximum(row_maxes, jnp.max(scores, axis=-1))
    weights = jnp.exp(scores - new_maxes[..., None])
    rescale = jnp.exp(row_maxes - new_maxes)
    totals = totals * rescale + jnp.sum(weights, axis=-1)
    accumulated = accumulated * rescale[..., None] + jnp.einsum(
        "hgqk,khd->hgqd",
        weights.astype(jnp.bfloat16),
        valued_rows,
        preferred_element_type=jnp.float32,
    )
    return (new_maxes, totals, accumulated)


def attend_slots(
    slot_queries,
    slot_sources,
    slot_starts,
    slot_lengths,
    active_count,
    key_stack,
    value_stack,
    prefix_keys,
    prefix_values,
):
    slot_total = slot_queries.shape[0]
    block_rows = slot_queries.shape[1]
    kv_heads = prefix_keys.shape[1] // HD
    group_size = HQ // KVH
    stat_shape = (slot_total, kv_heads, group_size, block_rows)
    initial = (
        jnp.full(stat_shape, -jnp.inf, jnp.float32),
        jnp.zeros(stat_shape, jnp.float32),
        jnp.zeros(stat_shape + (HD,), jnp.float32),
    )

    def per_slot(state_all, slot_index, key_rows, value_rows, visible):
        picked = jax.tree.map(
            lambda stacked: lax.dynamic_index_in_dim(stacked, slot_index, 0, keepdims=False),
            state_all,
        )
        query_block = lax.dynamic_index_in_dim(slot_queries, slot_index, 0, keepdims=False)
        updated = update(picked, query_block, key_rows, value_rows, visible)
        return jax.tree.map(
            lambda stacked, fresh_state: lax.dynamic_update_index_in_dim(
                stacked, fresh_state, slot_index, 0
            ),
            state_all,
            updated,
        )

    shard_pieces = (
        lax.all_gather(prefix_keys, "sample", axis=0, tiled=True),
        lax.all_gather(prefix_values, "sample", axis=0, tiled=True),
    )

    def step_slot(slot_index, state_inner):
        return per_slot(state_inner, slot_index, shard_pieces[0], shard_pieces[1], None)

    state_all = lax.fori_loop(0, active_count, step_slot, initial)
    suffix_total = key_stack.shape[1]

    def suffix_slot(slot_index, state_inner):
        source = slot_sources[slot_index]
        key_rows = lax.dynamic_index_in_dim(key_stack, source, 0, keepdims=False)
        value_rows = lax.dynamic_index_in_dim(value_stack, source, 0, keepdims=False)
        row_ids = slot_starts[slot_index] + jnp.arange(block_rows, dtype=jnp.int32)
        visible = jnp.arange(suffix_total, dtype=jnp.int32)[None, :] <= row_ids[:, None]
        return per_slot(state_inner, slot_index, key_rows, value_rows, visible)

    row_maxes, totals, accumulated = lax.fori_loop(0, active_count, suffix_slot, state_all)
    slot_ids = jnp.arange(slot_total, dtype=jnp.int32)
    row_ids = slot_starts[:, None] + jnp.arange(block_rows, dtype=jnp.int32)[None, :]
    live_rows = (row_ids < slot_lengths[:, None]) & (slot_ids[:, None] < active_count)
    live_stat = live_rows[:, None, None, :]
    normalized = accumulated / jnp.where(live_stat, totals, 1.0)[..., None]
    normalized = jnp.where(live_stat[..., None], normalized, 0.0)
    arranged = jnp.transpose(normalized, (0, 3, 1, 2, 4)).reshape(
        slot_total, block_rows, kv_heads * group_size * HD
    )
    return arranged.astype(jnp.bfloat16)


def per_device(
    queries, suffix_keys, suffix_values, prefix_keys, prefix_values, lengths, out_weight
):
    block_rows = BLK
    suffix_rows = queries.shape[1]
    query_width = queries.shape[2]
    block_count = suffix_rows // block_rows
    own_blocks = queries[0].reshape(block_count, block_rows, query_width)
    my_index = lax.axis_index("sample")
    own_length = lengths[my_index]
    own_needed = (own_length + block_rows - 1) // block_rows
    block_ids = jnp.arange(block_count, dtype=jnp.int32)
    slot_sources = jnp.zeros((block_count,), jnp.int32)
    slot_lengths = jnp.zeros((block_count,), jnp.int32) + own_length
    merged = attend_slots(
        own_blocks,
        slot_sources,
        block_ids * block_rows,
        slot_lengths,
        own_needed,
        suffix_keys,
        suffix_values,
        prefix_keys,
        prefix_values,
    )
    row_ids = jnp.arange(suffix_rows, dtype=jnp.int32)
    attended = jnp.where(
        (row_ids < own_length)[:, None],
        merged.reshape(suffix_rows, query_width),
        jnp.zeros((), jnp.bfloat16),
    )
    partial_rows = jnp.dot(
        attended,
        lax.all_gather(out_weight, "sample", axis=1, tiled=True),
        preferred_element_type=jnp.float32,
    )
    summed = lax.psum_scatter(
        partial_rows.astype(jnp.bfloat16), "head", scatter_dimension=0, tiled=True
    )
    return summed[None]


def solution(mesh):
    placed = (
        P("sample", None, "head"),
        P("sample", None, "head"),
        P("sample", None, "head"),
        P("sample", "head"),
        P("sample", "head"),
        P(),
        P("head", "sample"),
    )
    return jax.shard_map(
        per_device, mesh=mesh, in_specs=placed, out_specs=P("sample", "head", None), check_vma=False
    )
```

profile of v0, /device:TPU:1, one launch (start us, length us, event | category | flops | bytes accessed | tf_op | source)
XLA Modules:
  0.0 371.1 jit_solution(1939083098513244572)
XLA Ops:
  12.1 33.1 %all-gather.4.cloned.1.call-done = bf16[4096,128]{1,0:T(8,128)(2,1)} async-done(((bf16[256,128]{1,0:T(8,128)(2,1)}), bf16[4096,128]{1,0:T(8,128)(2,1)}) %all-gather.4.cloned.1.call-update) | async-done | bytes 1048592 | tf_op jit(solution)/shard_map/all_gather | solution.py:74
  45.2 34.2 %all-gather.6.cloned.1.call-done = bf16[4096,128]{1,0:T(8,128)(2,1)} async-done(((bf16[256,128]{1,0:T(8,128)(2,1)}), bf16[4096,128]{1,0:T(8,128)(2,1)}) %all-gather.6.cloned.1.call-update) | async-done | bytes 1048592 | tf_op jit(solution)/shard_map/all_gather | solution.py:75
  81.2 119.3 %while.28 = (s32[]{:T(128)}, f32[8,1,8,64]{2,3,1,0:T(8,128)}, f32[8,1,8,64]{2,3,1,0:T(8,128)}, f32[8,1,8,64,128]{4,3,2,1,0:T(8,128)S(1)}, s32[]{:T(128)}, /*inde...) while((s32[]{:T(128)}, f32[8,1,8,64]{2,3,1,0:T(8,128)}, ...), condition=%wide.region_3.4_spmd, body=%wide.region_0.3_spmd.sunk | while | flops 1090652160 | bytes 67399904 | solution.py:81
  82.2 2.6 bitcast_reduce_fusion.2
  85.6 2.5 copy-done
  89.7 5.1 %fusion.56 = f32[8,64]{0,1:T(8,128)S(1)} fusion(f32[64,8,4096]{2,1,0:T(8,128)} %copy-done, f32[8,64]{0,1:T(8,128)S(1)} %get-tuple-element.265), kind=kLoop, calls=%fused_computation.4.clone.1 | loop fusion | flops 6290944 | bytes 8392704 | tf_op jit(solution)/shard_map/while/body/reduce_sum | solution.py:26
  97.2 2.6 bitcast_reduce_fusion.2
  100.6 2.5 copy-done
  104.7 5.1 %fusion.56 = f32[8,64]{0,1:T(8,128)S(1)} fusion(f32[64,8,4096]{2,1,0:T(8,128)} %copy-done, f32[8,64]{0,1:T(8,128)S(1)} %get-tuple-element.265), kind=kLoop, calls=%fused_computation.4.clone.1 | loop fusion | flops 6290944 | bytes 8392704 | tf_op jit(solution)/shard_map/while/body/reduce_sum | solution.py:26
  112.2 2.6 bitcast_reduce_fusion.2
  115.7 2.5 copy-done
  119.8 5.0 %fusion.56 = f32[8,64]{0,1:T(8,128)S(1)} fusion(f32[64,8,4096]{2,1,0:T(8,128)} %copy-done, f32[8,64]{0,1:T(8,128)S(1)} %get-tuple-element.265), kind=kLoop, calls=%fused_computation.4.clone.1 | loop fusion | flops 6290944 | bytes 8392704 | tf_op jit(solution)/shard_map/while/body/reduce_sum | solution.py:26
  124.8 1.4 fusion.57
  127.2 2.6 bitcast_reduce_fusion.2
  130.7 2.5 copy-done
  134.8 5.0 %fusion.56 = f32[8,64]{0,1:T(8,128)S(1)} fusion(f32[64,8,4096]{2,1,0:T(8,128)} %copy-done, f32[8,64]{0,1:T(8,128)S(1)} %get-tuple-element.265), kind=kLoop, calls=%fused_computation.4.clone.1 | loop fusion | flops 6290944 | bytes 8392704 | tf_op jit(solution)/shard_map/while/body/reduce_sum | solution.py:26
  142.2 2.6 bitcast_reduce_fusion.2
  145.6 2.5 copy-done
  149.7 4.9 %fusion.56 = f32[8,64]{0,1:T(8,128)S(1)} fusion(f32[64,8,4096]{2,1,0:T(8,128)} %copy-done, f32[8,64]{0,1:T(8,128)S(1)} %get-tuple-element.265), kind=kLoop, calls=%fused_computation.4.clone.1 | loop fusion | flops 6290944 | bytes 8392704 | tf_op jit(solution)/shard_map/while/body/reduce_sum | solution.py:26
  157.0 2.6 bitcast_reduce_fusion.2
  160.4 2.5 copy-done
  164.5 4.9 %fusion.56 = f32[8,64]{0,1:T(8,128)S(1)} fusion(f32[64,8,4096]{2,1,0:T(8,128)} %copy-done, f32[8,64]{0,1:T(8,128)S(1)} %get-tuple-element.265), kind=kLoop, calls=%fused_computation.4.clone.1 | loop fusion | flops 6290944 | bytes 8392704 | tf_op jit(solution)/shard_map/while/body/reduce_sum | solution.py:26
  171.9 2.6 bitcast_reduce_fusion.2
  175.3 2.5 copy-done
  179.4 4.9 %fusion.56 = f32[8,64]{0,1:T(8,128)S(1)} fusion(f32[64,8,4096]{2,1,0:T(8,128)} %copy-done, f32[8,64]{0,1:T(8,128)S(1)} %get-tuple-element.265), kind=kLoop, calls=%fused_computation.4.clone.1 | loop fusion | flops 6290944 | bytes 8392704 | tf_op jit(solution)/shard_map/while/body/reduce_sum | solution.py:26
  186.7 2.6 bitcast_reduce_fusion.2
  190.1 2.5 copy-done
  194.2 4.9 %fusion.56 = f32[8,64]{0,1:T(8,128)S(1)} fusion(f32[64,8,4096]{2,1,0:T(8,128)} %copy-done, f32[8,64]{0,1:T(8,128)S(1)} %get-tuple-element.265), kind=kLoop, calls=%fused_computation.4.clone.1 | loop fusion | flops 6290944 | bytes 8392704 | tf_op jit(solution)/shard_map/while/body/reduce_sum | solution.py:26
  200.5 59.3 %while.29 = (s32[]{:T(128)}, f32[8,1,8,64]{2,3,1,0:T(8,128)}, f32[8,1,8,64]{2,3,1,0:T(8,128)}, f32[8,1,8,64,128]{4,3,2,1,0:T(8,128)S(1)}, s32[]{:T(128)}, /*inde...) while((s32[]{:T(128)}, f32[8,1,8,64]{2,3,1,0:T(8,128)}, ...), condition=%wide.region_7.8_spmd, body=%wide.region_4.7_spmd.sunk | while | flops 135956544 | bytes 5335739 | solution.py:92
  221.3 1.4 fusion.65
  262.6 11.5 %convolution_convert_fusion = bf16[512,5120]{1,0:T(8,128)(2,1)} fusion(bf16[1024,5120]{0,1:T(8,128)(2,1)} %all-gather.8.cloned.1.call-done, bf16[64,8,8,128]{3,2,1,0:T(8,128)(2,1)S(1)} %bitcast.175, pred[512]{0:T(512)(128)(4,1)S(1)} %iota_compare_fusion.1), kind=kOutput, calls=%fused_computation.48 | convolution fusion | flops 5371854848 | bytes 16777728 | tf_op jit(solution)/shard_map/dot_general | solution.py:136
  274.1 90.5 %reduce-scatter.2.cloned.1.call-done = bf16[64,5120]{1,0:T(8,128)(2,1)} async-done(((bf16[512,5120]{1,0:T(8,128)(2,1)}), bf16[64,5120]{1,0:T(8,128)(2,1)}) %reduce-scatter.2.cloned.1.call-update) | async-done | bytes 655376 | tf_op jit(solution)/shard_map/reduce_scatter | solution.py:141
  (203 shorter events, 104.0 us)
Async XLA Ops:
  6.5 38.7 %all-gather.4.cloned.1.call-start = ((), (), s32[]{:S(2)}) async-start(), calls=%async_computation.1 | async-start | bytes 1114112 | tf_op jit(solution)/shard_map/all_gather | solution.py:74
  7.3 72.2 %all-gather.6.cloned.1.call-start = ((), (), s32[]{:S(2)}) async-start(), calls=%async_computation.2 | async-start | bytes 1114112 | tf_op jit(solution)/shard_map/all_gather | solution.py:75
  8.0 254.5 %all-gather.8.cloned.1.call-start = ((), (), s32[]{:S(2)}) async-start(), calls=%async_computation.3 | async-start | bytes 11141120 | tf_op jit(solution)/shard_map/all_gather | solution.py:138
  8.7 355.9 %reduce-scatter.2.cloned.1.call-start = ((), (), s32[]{:S(2)}) async-start(), calls=%async_computation.4 | async-start | bytes 5898240 | tf_op jit(solution)/shard_map/reduce_scatter | solution.py:141
  81.2 7.0 %copy-start.1 = (bf16[4096,128]{1,0:T(8,128)(2,1)S(1)}, bf16[4096,128]{1,0:T(8,128)(2,1)}, u32[]{:S(2)}) copy-start(bf16[4096,128]{1,0:T(8,128)(2,1)} %get-tuple-element.315) | copy-start | bytes 3145732 | tf_op jit(solution)/shard_map/while
  84.8 3.3 copy-start
  96.2 7.0 %copy-start.1 = (bf16[4096,128]{1,0:T(8,128)(2,1)S(1)}, bf16[4096,128]{1,0:T(8,128)(2,1)}, u32[]{:S(2)}) copy-start(bf16[4096,128]{1,0:T(8,128)(2,1)} %get-tuple-element.315) | copy-start | bytes 3145732 | tf_op jit(solution)/shard_map/while
  99.8 3.3 copy-start
  111.2 7.0 %copy-start.1 = (bf16[4096,128]{1,0:T(8,128)(2,1)S(1)}, bf16[4096,128]{1,0:T(8,128)(2,1)}, u32[]{:S(2)}) copy-start(bf16[4096,128]{1,0:T(8,128)(2,1)} %get-tuple-element.315) | copy-start | bytes 3145732 | tf_op jit(solution)/shard_map/while
  114.8 3.3 copy-start
  126.2 7.0 %copy-start.1 = (bf16[4096,128]{1,0:T(8,128)(2,1)S(1)}, bf16[4096,128]{1,0:T(8,128)(2,1)}, u32[]{:S(2)}) copy-start(bf16[4096,128]{1,0:T(8,128)(2,1)} %get-tuple-element.315) | copy-start | bytes 3145732 | tf_op jit(solution)/shard_map/while
  129.9 3.3 copy-start
  141.2 6.9 %copy-start.1 = (bf16[4096,128]{1,0:T(8,128)(2,1)S(1)}, bf16[4096,128]{1,0:T(8,128)(2,1)}, u32[]{:S(2)}) copy-start(bf16[4096,128]{1,0:T(8,128)(2,1)} %get-tuple-element.315) | copy-start | bytes 3145732 | tf_op jit(solution)/shard_map/while
  144.8 3.3 copy-start
  156.0 7.0 %copy-start.1 = (bf16[4096,128]{1,0:T(8,128)(2,1)S(1)}, bf16[4096,128]{1,0:T(8,128)(2,1)}, u32[]{:S(2)}) copy-start(bf16[4096,128]{1,0:T(8,128)(2,1)} %get-tuple-element.315) | copy-start | bytes 3145732 | tf_op jit(solution)/shard_map/while
  159.6 3.3 copy-start
  170.8 7.0 %copy-start.1 = (bf16[4096,128]{1,0:T(8,128)(2,1)S(1)}, bf16[4096,128]{1,0:T(8,128)(2,1)}, u32[]{:S(2)}) copy-start(bf16[4096,128]{1,0:T(8,128)(2,1)} %get-tuple-element.315) | copy-start | bytes 3145732 | tf_op jit(solution)/shard_map/while
  174.4 3.3 copy-start
  185.7 6.9 %copy-start.1 = (bf16[4096,128]{1,0:T(8,128)(2,1)S(1)}, bf16[4096,128]{1,0:T(8,128)(2,1)}, u32[]{:S(2)}) copy-start(bf16[4096,128]{1,0:T(8,128)(2,1)} %get-tuple-element.315) | copy-start | bytes 3145732 | tf_op jit(solution)/shard_map/while
  189.3 3.3 copy-start
Sparse Core Ops, SparseCore 0:
  9.1 36.1 all-gather.3
  46.9 32.5 all-gather.5
  81.2 62.0 all-gather.7
  274.2 90.3 reduce-scatter.1
where the time goes:
time: 375 us; the launch traced here: 371 us
  waiting for transfers between devices  160 us (43%)
  other arithmetic  87.4 us (23%)
  matrix products  63.3 us (17%)
  local copies, waits for them, and re-layouts  45.6 us (12%)
  between operations  13.9 us (4%)
    reduce_scatter x1, waiting for transfers between devices, per_device(): lax.psum_scatter(partial_rows.astype(jnp.bfloat16), 'head', scatter_dimen...  90.5 us
    reduce_sum x8, other arithmetic, update(): totals = totals * rescale + jnp.sum(weights, axis=-1)  39.6 us
    while x64, local copies, waits for them, and re-layouts  35.8 us
    all_gather x1, waiting for transfers between devices, attend_slots(): lax.all_gather(prefix_values, 'sample', axis=0, tiled=True)  34.2 us
    all_gather x1, waiting for transfers between devices, attend_slots(): lax.all_gather(prefix_keys, 'sample', axis=0, tiled=True)  33.1 us
    dot_general x16, matrix products, update(): jnp.einsum('qhgd,khd->hgqk', grouped, keyed_rows, preferred_element_type=...  31.2 us
    dynamic_update_slice x24, other arithmetic, per_slot(): lax.dynamic_update_index_in_dim(stacked, fresh_state, slot_index, 0)  23.7 us
    dot_general x16, matrix products, update(): jnp.einsum('hgqk,khd->hgqd', weights.astype(jnp.bfloat16), valued_rows, p...  20.6 us
  transfers between devices with their start and end apart: 4, of which 3 were waited for; matrix products, arithmetic and copies ran while one was open for 44% of the time, Pallas kernels for 0%

commit v1 on v0

v1 whole, which is shorter than its diff:
```python
import functools
import math

import jax
import jax.numpy as jnp
from jax import lax
from jax.experimental import pallas as pl
from jax.experimental.pallas import tpu as pltpu
from jax.sharding import PartitionSpec as P

HD = 128
HEADS = 4
TILE = 256
SCALE = HD ** (-0.5) * math.log2(math.e)
BF = jnp.bfloat16
F32 = jnp.float32
NT = (((1,), (1,)), ((), ()))


def sample_pairs(to):
    place = lambda z, y, c: (z * 4 + y) * 2 + c
    return [
        (place(z, y, c), place(*to(z, y, c)))
        for z in range(2) for y in range(4) for c in range(2)
    ]


def head_pairs(to):
    pairs = []
    for x in range(4):
        for z in range(2):
            tx, tz = to(x, z)
            pairs.append((x * 2 + z, tx * 2 + tz))
    return pairs


CORE = sample_pairs(lambda z, y, c: (z, y, 1 - c))
ZLO = sample_pairs(lambda z, y, c: (1 - z, y, c))
YUP = sample_pairs(lambda z, y, c: (z, (y + 1) % 4, c))
YDOWN = sample_pairs(lambda z, y, c: (z, (y + 3) % 4, c))
YFAR = sample_pairs(lambda z, y, c: (z, (y + 2) % 4, c))
XUP = head_pairs(lambda x, z: ((x + 1) % 4, z))
XDOWN = head_pairs(lambda x, z: ((x + 3) % 4, z))
ZHI = head_pairs(lambda x, z: (x, 1 - z))


def over_sample(value, pairs):
    return lax.ppermute(value, "sample", pairs)


def over_head(value, pairs):
    return lax.ppermute(value, "head", pairs)


def attend_kernel(counts, first, last, lens_ref, q_ref, *refs):
    refs = list(refs)
    suffix_ref = refs.pop(0) if first else None
    kv_refs = [refs.pop(0) for _ in counts]
    acc_in, stat_in = (None, None) if first else (refs.pop(0), refs.pop(0))
    if last:
        out_ref = refs.pop(0)
    else:
        acc_out, stat_out = refs.pop(0), refs.pop(0)
    keys_ref, values_ref = refs.pop(0), refs.pop(0)
    sample, tile = pl.program_id(0), pl.program_id(1)
    rows_total = keys_ref.shape[0]

    @pl.when((sample == 0) & (tile == 0))
    def _():
        at = 0
        for kv_ref, count in zip(kv_refs, counts):
            for b in range(count):
                block = kv_ref[b]
                rows = block.shape[0]
                keys_ref[at:at + rows] = block[:, :HD]
                values_ref[at:at + rows, :HD] = block[:, HD:]
                at += rows
        values_ref[:, HD:] = jnp.ones((rows_total, HD), BF)

    length = lens_ref[sample]
    live = tile * TILE < length

    def fold(state, scores, values):
        top = jnp.max(scores, axis=1, keepdims=True)
        if state is None:
            weights = jnp.exp2(scores - top)
            return top, jnp.dot(weights.astype(BF), values, preferred_element_type=F32)
        old, acc = state
        top = jnp.maximum(old, top)
        weights = jnp.exp2(scores - top)
        part = jnp.dot(weights.astype(BF), values, preferred_element_type=F32)
        return top, acc * jnp.exp2(old - top) + part

    def body(tile_static):
        for h in range(HEADS):
            cols = slice(h * HD, (h + 1) * HD)
            q = (q_ref[:, cols].astype(F32) * SCALE).astype(BF)
            if first:
                row = lax.broadcasted_iota(jnp.int32, (TILE, TILE), 0)
                col = lax.broadcasted_iota(jnp.int32, (TILE, TILE), 1)
                state = None
                for t in range(tile_static, -1, -1):
                    block = suffix_ref[t * TILE:(t + 1) * TILE]
                    scores = lax.dot_general(q, block[:, :HD], NT, preferred_element_type=F32)
                    if t == tile_static:
                        scores = jnp.where(col <= row, scores, -1e30)
                    values = jnp.concatenate([block[:, HD:], jnp.ones((TILE, HD), BF)], 1)
                    state = fold(state, scores, values)
            else:
                state = None
            at = 0
            while at < rows_total:
                size = TILE if first else rows_total
                scores = lax.dot_general(q, keys_ref[at:at + size], NT, preferred_element_type=F32)
                state = fold(state, scores, values_ref[at:at + size])
                at += size
            top, acc = state
            num, den = acc[:, :HD], acc[:, HD:]
            if not first:
                top = jnp.broadcast_to(top, (TILE, HD))
                old = jnp.broadcast_to(stat_in[:, h:h + 1], (TILE, HD))
                total = jnp.broadcast_to(stat_in[:, HEADS + h:HEADS + h + 1], (TILE, HD))
                new = jnp.maximum(old, top)
                keep, add = jnp.exp2(old - new), jnp.exp2(top - new)
                num = acc_in[:, cols] * keep + num * add
                den = total * keep + den * add
                top = new[:, :1]
            if last:
                row = tile * TILE + lax.broadcasted_iota(jnp.int32, (TILE, HD), 0)
                out_ref[:, cols] = jnp.where(row < length, num / den, 0.0).astype(BF)
            else:
                acc_out[:, cols] = num
                stat_out[:, h:h + 1] = top
                stat_out[:, HEADS + h:HEADS + h + 1] = den[:, :1]

    if first:
        for t in range(2):
            pl.when(live & (tile == t))(functools.partial(body, t))
    else:
        pl.when(live)(functools.partial(body, 0))

    if last:
        @pl.when(jnp.logical_not(live))
        def _():
            out_ref[...] = jnp.zeros_like(out_ref)


def attend(lens, q, suffix, kvs, state, last):
    first = state is None
    samples, rows, width = q.shape
    counts = [kv.shape[0] for kv in kvs]
    keys_total = sum(kv.shape[0] * kv.shape[1] for kv in kvs)
    tiled = lambda w: pl.BlockSpec((None, TILE, w), lambda s, t, _: (s, t, 0))
    in_specs = [tiled(width)]
    args = [q]
    if first:
        in_specs.append(pl.BlockSpec((None, rows, 2 * HD), lambda s, t, _: (s, 0, 0)))
        args.append(suffix)
    for kv in kvs:
        in_specs.append(pl.BlockSpec(kv.shape, lambda s, t, _: (0, 0, 0)))
        args.append(kv)
    if not first:
        in_specs += [tiled(width), tiled(HD)]
        args += list(state)
    if last:
        out_specs = tiled(width)
        out_shape = jax.ShapeDtypeStruct((samples, rows, width), BF)
    else:
        out_specs = [tiled(width), tiled(HD)]
        out_shape = [
            jax.ShapeDtypeStruct((samples, rows, width), F32),
            jax.ShapeDtypeStruct((samples, rows, HD), F32),
        ]
    keys_seen = keys_total + (rows // 2 if first else 0)
    return pl.pallas_call(
        functools.partial(attend_kernel, counts, first, last),
        grid_spec=pltpu.PrefetchScalarGridSpec(
            num_scalar_prefetch=1,
            grid=(samples, rows // TILE),
            in_specs=in_specs,
            out_specs=out_specs,
            scratch_shapes=[
                pltpu.VMEM((keys_total, HD), BF),
                pltpu.VMEM((keys_total, 2 * HD), BF),
            ],
        ),
        out_shape=out_shape,
        name="attend_first" if first else "attend_last" if last else "attend_more",
        cost_estimate=pl.CostEstimate(
            flops=samples * rows * HEADS * keys_seen * HD * 8,
            bytes_accessed=8 * 2**20,
            transcendentals=samples * rows * HEADS * keys_seen,
        ),
        compiler_params=pltpu.CompilerParams(vmem_limit_bytes=48 * 2**20),
    )(lens, *args)


def project_kernel(count, spans, place_ref, w_own_ref, w_other_ref, *refs):
    own_refs, other_refs = refs[:count], refs[count:2 * count]
    add_refs, out_ref = refs[2 * count:-1], refs[-1]
    tile = pl.program_id(0)
    own = jnp.concatenate([ref[s] for ref in own_refs for s in (0, 1)], axis=0)
    other = jnp.concatenate([ref[s] for ref in other_refs for s in (1, 0)], axis=0)
    acc = lax.dot_general(w_own_ref[...], own, NT, preferred_element_type=F32)
    acc = acc + lax.dot_general(w_other_ref[...], other, NT, preferred_element_type=F32)
    partial = []
    for ref, (_, start, tiles, whole) in zip(add_refs, spans):
        if whole:
            acc = acc + ref[...].astype(F32)
        else:
            partial.append((ref, start, tiles))
    out_ref[...] = acc.astype(BF)
    for ref, start, tiles in partial:
        @pl.when((tile >= start) & (tile < start + tiles))
        def _():
            out_ref[...] = (acc + ref[...].astype(F32)).astype(BF)


def project(place, weight, rows_own, rows_other, first, tiles, size, blocks, adds, name):
    depth = rows_own.shape[3]
    lanes = 2 * rows_own.shape[2] * len(blocks)

    def rows_spec(step, own):
        def index(i, p):
            z = p[1] if own else 1 - p[1]
            return (0, 2 * lax.rem(p[0] + step, 4) + z, 0, 0)

        return pl.BlockSpec((2, None, rows_own.shape[2], depth), index)

    def add_spec(lane, start, count):
        return pl.BlockSpec(
            (size, lanes), lambda i, p: (jnp.clip(i - start, 0, count - 1), lane)
        )

    spans = [(lane, start, count, count == tiles) for _, lane, start, count in adds]
    in_specs = [
        pl.BlockSpec((size, depth), lambda i, p: (first + i, p[2])),
        pl.BlockSpec((size, depth), lambda i, p: (first + i, 1 - p[2])),
    ]
    in_specs += [rows_spec(*block) for block in blocks] * 2
    in_specs += [add_spec(lane, start, count) for _, lane, start, count in adds]
    return pl.pallas_call(
        functools.partial(project_kernel, len(blocks), spans),
        grid_spec=pltpu.PrefetchScalarGridSpec(
            num_scalar_prefetch=1,
            grid=(tiles,),
            in_specs=in_specs,
            out_specs=pl.BlockSpec((size, lanes), lambda i, p: (i, 0)),
        ),
        out_shape=jax.ShapeDtypeStruct((tiles * size, lanes), BF),
        name=name,
        cost_estimate=pl.CostEstimate(
            flops=4 * tiles * size * lanes * depth,
            bytes_accessed=4 * tiles * size * depth + 2 * tiles * size * lanes,
            transcendentals=0,
        ),
        compiler_params=pltpu.CompilerParams(vmem_limit_bytes=32 * 2**20),
    )(place, weight, weight, *([rows_own] * len(blocks)), *([rows_other] * len(blocks)), *[a[0] for a in adds])


def finish_kernel(cols, place_ref, own_ref, got_ref, out_ref):
    own = own_ref[...].astype(F32)[:, :64]
    got = got_ref[...].astype(F32)[:, 64:]
    first = place_ref[2] == 0
    even = jnp.where(first, own, got)
    odd = jnp.where(first, got, own)
    both = jnp.concatenate([even, odd], axis=0)
    out_ref[...] = jnp.transpose(both).astype(BF)


def finish(place, own, got, cols):
    blocks = own.shape[0] // cols
    part = pl.BlockSpec((cols, 128), lambda i, p: (i, 0))
    return pl.pallas_call(
        functools.partial(finish_kernel, cols),
        grid_spec=pltpu.PrefetchScalarGridSpec(
            num_scalar_prefetch=1,
            grid=(blocks,),
            in_specs=[part, part],
            out_specs=pl.BlockSpec((64, 2 * cols), lambda i, p: (0, i)),
        ),
        out_shape=jax.ShapeDtypeStruct((64, 2 * cols * blocks), BF),
        name="finish",
    )(place, own, got)


PARITY = [[i for i in range(16) if i % 2 == c] for c in range(2)]
SIZE = 256
EARLY, LATE = 6, 4


def per_device(
    queries, suffix_keys, suffix_values, prefix_keys, prefix_values, lengths, out_weight
):
    sample = lax.axis_index("sample")
    head = lax.axis_index("head")
    core = sample % 2
    x, z_hi = head // 2, head % 2
    place = jnp.stack([x, z_hi, core]).astype(jnp.int32)

    weight = lax.all_gather(out_weight.T, "sample", axis=0, tiled=True, axis_index_groups=PARITY)

    lens = jnp.stack([lengths[sample], lengths[sample + 1 - 2 * core]])
    kv = jnp.concatenate([prefix_keys, prefix_values], axis=1)
    suffix = jnp.concatenate([suffix_keys[0], suffix_values[0]], axis=1)
    width = queries.shape[2] // 2
    mine = lax.dynamic_slice_in_dim(queries[0], core * width, width, axis=1)
    theirs = lax.dynamic_slice_in_dim(queries[0], (1 - core) * width, width, axis=1)

    kv_z = over_sample(kv, ZLO)
    kv_core = over_sample(kv, CORE)
    q = jnp.stack([mine, over_sample(theirs, CORE)])
    suffixes = jnp.stack([suffix, over_sample(suffix, CORE)])
    near = jnp.stack([kv, kv_z])
    ys = [over_sample(near, to) for to in (YUP, YDOWN, YFAR)]

    state = attend(lens, q, suffixes, [jnp.stack([kv, kv_core])], None, False)
    ys, state = lax.optimization_barrier((ys, state))
    rest = [kv_z[None]] + ys
    rest_core = [over_sample(block, CORE) for block in rest]
    state = attend(lens, q, None, rest, state, False)
    half = attend(lens, q, None, rest_core, state, True)

    half_core = over_sample(half, CORE)
    half = half.reshape(2, 8, 64, width)
    half_core = half_core.reshape(2, 8, 64, width)

    def early(blocks, adds, name):
        return project(place, weight, half, half_core, 0, EARLY, SIZE, blocks, adds, name)

    def late(blocks, adds, name):
        return project(place, weight, half, half_core, EARLY, LATE, SIZE, blocks, adds, name)

    def halves(array):
        lines = array.shape[0] // 2
        return over_head(array[:lines], XUP), over_head(array[lines:], XDOWN)

    OTHER, OWN = False, True
    both_z = lambda step: [(step, OTHER), (step, OWN)]
    he, hl = EARLY // 2, LATE // 2

    got = over_head(late([(s, OTHER) for s in range(4)], [], "late_give"), ZHI)
    via_up, via_down = halves(early(both_z(2), [], "early_far"))
    below = over_head(early(both_z(1), [(via_up, 0, 0, he)], "early_up"), XUP)
    above = over_head(early(both_z(3), [(via_down, 0, he, he)], "early_down"), XDOWN)
    lvia_up, lvia_down = halves(late([(2, OWN)], [(got, 2, 0, LATE)], "late_far"))
    whole = (0, EARLY)
    give = early([(0, OTHER)], [(below, 0, *whole), (above, 0, *whole)], "early_give")
    from_z = over_head(give, ZHI)
    lbelow = over_head(
        late([(1, OWN)], [(got, 1, 0, LATE), (lvia_up, 0, 0, hl)], "late_up"), XUP
    )
    labove = over_head(
        late([(3, OWN)], [(got, 3, 0, LATE), (lvia_down, 0, hl, hl)], "late_down"), XDOWN
    )
    early_sum = early(
        [(0, OWN)], [(below, 1, *whole), (above, 1, *whole), (from_z, 0, *whole)], "early_sum"
    )
    late_sum = late(
        [(0, OWN)], [(got, 0, 0, LATE), (lbelow, 0, 0, LATE), (labove, 0, 0, LATE)], "late_sum"
    )

    done = jnp.concatenate([early_sum, late_sum], axis=0)
    return finish(place, done, over_sample(done, CORE), out_weight.shape[1])[None]


def solution(mesh):
    placed = (
        P("sample", None, "head"),
        P("sample", None, "head"),
        P("sample", None, "head"),
        P("sample", "head"),
        P("sample", "head"),
        P(),
        P("head", "sample"),
    )
    return jax.shard_map(
        per_device, mesh=mesh, in_specs=placed, out_specs=P("sample", "head", None), check_vma=False
    )
```

time: 375 us -> 174 us (0.46); the launches traced: 371 us -> 174 us
  waiting for transfers between devices: 160 us -> 49.1 us
  other arithmetic: 87.4 us -> 1.69 us
  Pallas kernels: 0 us -> 66.6 us
  matrix products: 63.3 us -> 0 us
  local copies, waits for them, and re-layouts: 45.6 us -> 6.75 us
  starting transfers between devices: 0.12 us -> 36.1 us
    reduce_scatter x1 -> x0, waiting for transfers between devices: 90.5 us -> none  [per_device(): lax.psum_scatter(partial_rows.astype(jnp.bfloat16), 'head', scatter_dimen...]
    pallas_call x0 -> x14, Pallas kernels: none -> 66.6 us  [the longest x3 32.4 us: attend(): pl.pallas_call(functools.partial(attend_kernel, counts, first, last), gri...]
    dot_general x33 -> x0, matrix products: 63.3 us -> none  [the longest x16 31.2 us: update(): jnp.einsum('qhgd,khd->hgqk', grouped, keyed_rows, preferred_element_type=...]
    all_gather x3 -> x1, waiting for transfers between devices: 67.4 us -> 10.8 us  [per_device(): lax.all_gather(out_weight.T, 'sample', axis=0, tiled=True, axis_index_gro...]
    reduce_sum x8 -> x0, other arithmetic: 39.6 us -> none  [update(): totals = totals * rescale + jnp.sum(weights, axis=-1)]
    ppermute x0 -> x23, waiting for transfers between devices: none -> 37.6 us  [the longest x10 26.4 us: over_head(): return lax.ppermute(value, 'head', pairs)]
    ppermute x0 -> x23, starting transfers between devices: none -> 36 us  [the longest x13 21.5 us: over_sample(): return lax.ppermute(value, 'sample', pairs)]
    while x64 -> x0, local copies, waits for them, and re-layouts: 35.8 us -> none
  transfers between devices with their start and end apart: 4 -> 24, of which waited for: 3 -> 10; matrix products, arithmetic and copies ran while one was open for 44% -> 2% of each run, Pallas kernels for 0% -> 31%
where the time goes in v1:
time: 174 us
  Pallas kernels  66.6 us (38%)
  waiting for transfers between devices  49.1 us (28%)
  starting transfers between devices  36.1 us (21%)
  between operations  13.7 us (8%)
  local copies, waits for them, and re-layouts  6.75 us (4%)
    pallas_call x3, Pallas kernels, attend(): pl.pallas_call(functools.partial(attend_kernel, counts, first, last), gri...  32.4 us
    pallas_call x10, Pallas kernels, project(): pl.pallas_call(functools.partial(project_kernel, len(blocks), spans), gri...  27.4 us
    ppermute x10, waiting for transfers between devices, over_head(): return lax.ppermute(value, 'head', pairs)  26.4 us
    ppermute x13, starting transfers between devices, over_sample(): return lax.ppermute(value, 'sample', pairs)  21.5 us
    ppermute x10, starting transfers between devices, over_head(): return lax.ppermute(value, 'head', pairs)  14.6 us
    ppermute x13, waiting for transfers between devices, over_sample(): return lax.ppermute(value, 'sample', pairs)  11.2 us
    all_gather x1, waiting for transfers between devices, per_device(): lax.all_gather(out_weight.T, 'sample', axis=0, tiled=True, axis_index_gro...  10.8 us
    pallas_call x1, Pallas kernels, finish(): pl.pallas_call(functools.partial(finish_kernel, cols), grid_spec=pltpu.Pr...  6.82 us
  transfers between devices with their start and end apart: 24, of which 10 were waited for; matrix products, arithmetic and copies ran while one was open for 2% of the time, Pallas kernels for 31%

profile of v1, /device:TPU:1, one launch (start us, length us, event | category | flops | bytes accessed | tf_op | source)
XLA Modules:
  0.0 174.0 jit_solution(2026849887531581727)
XLA Ops:
  10.3 1.8 %collective-permute-start.1 = (bf16[256,256]{1,0:T(8,128)(2,1)S(1)}, bf16[256,256]{1,0:T(8,128)(2,1)S(1)}, u32[]{:S(2)}, u32[]{:S(2)}) collective-permute-start(bf16[256,256]{1,0:T(8,128)(2,1)S(1)} %constant_dynamic-update-slice_fusion), channel_id=1, source_target_pairs={{0,64},{8,72},{16,80},{24,88},{32,96},{40,104},{48,112},{56,120},{... | collective-permute-start | bytes 393224 | tf_op jit(solution)/shard_map/ppermute | solution.py:48
  18.4 1.6 collective-permute-start.5
  19.9 2.0 %collective-permute-start.2 = (bf16[1,256,256]{2,1,0:T(8,128)(2,1)S(1)}, bf16[1,256,256]{2,1,0:T(8,128)(2,1)S(1)}, u32[]{:S(2)}, u32[]{:S(2)}) collective-permute-start(bf16[1,256,256]{2,1,0:T(8,128)(2,1)S(1)} %bitcast.51), channel_id=1, source_target_pairs={{0,8},{8,0},{16,24},{24,16},{32,40},{40,32},{48,56},{56,48},{64,72... | collective-permute-start | bytes 393224 | tf_op jit(solution)/shard_map/ppermute | solution.py:48
  22.1 6.3 %attend_first.1 = (f32[2,512,512]{2,1,0:T(8,128)S(1)}, f32[2,512,128]{2,1,0:T(8,128)S(1)}) custom-call(s32[2]{0:T(128)S(1)} %pad_add_fusion.1.lens_ref, bf16[2,512,512]{2,1,0:T(8,128)(2,1)S(1)} %pad_maximum_fusion.q_ref, bf16[2,512,256]{2,1,0:T(8,128)(2,1)S(1)} %pad_maximum_fusion.2.refs_0_, bf16[2,256,256]{2,1,0:T(8,128)(2,1)S(1)} %get-tuple-element.31.refs_1_), custom_call_target="tpu_custom_call" | custom-call | flops 3221225472 | bytes 8388608 | tf_op jit(solution)/shard_map/attend_first/pallas_call | solution.py:175
  29.7 6.3 %collective-permute-done.5.refs_3_ = bf16[2,256,256]{2,1,0:T(8,128)(2,1)S(1)} collective-permute-done((bf16[2,256,256]{2,1,0:T(8,128)(2,1)S(1)}, bf16[2,256,256]{2,1,0:T(8,128)(2,1)S(1)}, u32[]{:S(2)}, u32[]{:S(2)}) %collective-permute-start.5) | collective-permute-done | bytes 262176 | tf_op jit(solution)/shard_map/ppermute | solution.py:48
  36.0 5.2 %collective-permute-start.10 = (bf16[2,256,256]{2,1,0:T(8,128)(2,1)S(1)}, bf16[2,256,256]{2,1,0:T(8,128)(2,1)S(1)}, u32[]{:S(2)}, u32[]{:S(2)}) collective-permute-start(bf16[2,256,256]{2,1,0:T(8,128)(2,1)S(1)} %collective-permute-done.5.refs_3_), channel_id=1, source_target_pairs={{0,8},{8,0},{16,24},{24,16},{32,40},{40,32},{48,56},{56,48},{64,72... | collective-permute-start | bytes 786440 | tf_op jit(solution)/shard_map/ppermute | solution.py:48
  41.8 13.7 %attend_more.1 = (f32[2,512,512]{2,1,0:T(8,128)S(1)}, f32[2,512,128]{2,1,0:T(8,128)S(1)}) custom-call(s32[2]{0:T(128)S(1)} %pad_add_fusion.1.lens_ref, bf16[2,512,512]{2,1,0:T(8,128)(2,1)S(1)} %pad_maximum_fusion.q_ref, bf16[1,256,256]{2,1,0:T(8,128)(2,1)S(1)} %bitcast.52, bf16[2,256,256]{2,1,0:T(8,128)(2,1)S(1)} %collective-permute-done.3.refs_1_, ...), custom_call_target="tpu_custom_call" | custom-call | flops 7516192768 | bytes 8388608 | tf_op jit(solution)/shard_map/attend_more/pallas_call | solution.py:175
  55.5 12.4 %attend_last.1 = bf16[2,512,512]{2,1,0:T(8,128)(2,1)S(1)} custom-call(s32[2]{0:T(128)S(1)} %pad_add_fusion.1.lens_ref, bf16[2,512,512]{2,1,0:T(8,128)(2,1)S(1)} %pad_maximum_fusion.q_ref, bf16[1,256,256]{2,1,0:T(8,128)(2,1)S(1)} %collective-permute-done.2.refs_0_, bf16[2,256,256]{2,1,0:T(8,128)(2,1)S(1)} %collective-permute-done.8.refs_1_, ...), custom_call_target="tpu_custom_call" | custom-call | flops 7516192768 | bytes 8388608 | tf_op jit(solution)/shard_map/attend_last/pallas_call | solution.py:175
  68.1 2.5 %collective-permute-done.11 = bf16[2,512,512]{2,1,0:T(8,128)(2,1)S(1)} collective-permute-done((bf16[2,512,512]{2,1,0:T(8,128)(2,1)S(1)}, bf16[2,512,512]{2,1,0:T(8,128)(2,1)S(1)}, u32[]{:S(2)}, u32[]{:S(2)}) %collective-permute-start.11) | collective-permute-done | bytes 1048608 | tf_op jit(solution)/shard_map/ppermute | solution.py:48
  70.7 10.8 %all-gather.2.cloned.1.call-done.w_own_ref.w_other_ref = bf16[2560,1024]{1,0:T(8,128)(2,1)} async-done(((bf16[320,1024]{1,0:T(8,128)(2,1)}), bf16[2560,1024]{1,0:T(8,128)(2,1)}) %all-gather.2.cloned.1.call-update) | async-done | bytes 5242896 | tf_op jit(solution)/shard_map/all_gather | solution.py:301
  81.5 2.5 %copy-done = bf16[2560,1024]{1,0:T(8,128)(2,1)S(1)} copy-done((bf16[2560,1024]{1,0:T(8,128)(2,1)S(1)}, bf16[2560,1024]{1,0:T(8,128)(2,1)}, u32[]{:S(2)}) %copy-start) | copy-done | bytes 5242904
  84.0 3.0 %late_give.1 = bf16[1024,512]{1,0:T(8,128)(2,1)S(1)} custom-call(s32[3]{0:T(128)S(1)} %pad_add_fusion.place_ref, bf16[2560,1024]{1,0:T(8,128)(2,1)S(1)} %copy-done, bf16[2560,1024]{1,0:T(8,128)(2,1)S(1)} %copy-done, bf16[2,8,64,512]{3,2,1,0:T(8,128)(2,1)S(1)} %bitcast.18, bf16[2,8,64,512]{3,2,1,0:T(8,128)(2,1)S(1)} %bitcast.19, ...), custom_call_target="tpu_custom_call" | custom-call | flops 1073741824 | bytes 3145728 | tf_op jit(solution)/shard_map/late_give/pallas_call | solution.py:242
  87.0 3.4 %collective-permute-start.17 = (bf16[1024,512]{1,0:T(8,128)(2,1)S(1)}, bf16[1024,512]{1,0:T(8,128)(2,1)S(1)}, u32[]{:S(2)}, u32[]{:S(2)}) collective-permute-start(bf16[1024,512]{1,0:T(8,128)(2,1)S(1)} %late_give.1), channel_id=1, source_target_pairs={{0,1},{1,0},{2,3},{3,2},{4,5},{5,4},{6,7},{7,6},{8,9},{9,8},{10,11... | collective-permute-start | bytes 3145736 | tf_op jit(solution)/shard_map/ppermute | solution.py:52
  90.4 3.1 %early_far.1 = bf16[1536,256]{1,0:T(8,128)(2,1)S(1)} custom-call(s32[3]{0:T(128)S(1)} %pad_add_fusion.place_ref, bf16[2560,1024]{1,0:T(8,128)(2,1)S(1)} %copy-done, bf16[2560,1024]{1,0:T(8,128)(2,1)S(1)} %copy-done, bf16[2,8,64,512]{3,2,1,0:T(8,128)(2,1)S(1)} %bitcast.22, bf16[2,8,64,512]{3,2,1,0:T(8,128)(2,1)S(1)} %bitcast.23, ...), custom_call_target="tpu_custom_call" | custom-call | flops 805306368 | bytes 3932160 | tf_op jit(solution)/shard_map/early_far/pallas_call | solution.py:242
  93.5 2.5 %collective-permute-start.14 = (bf16[768,256]{1,0:T(8,128)(2,1)S(1)}, bf16[768,256]{1,0:T(8,128)(2,1)S(1)}, u32[]{:S(2)}, u32[]{:S(2)}) collective-permute-start(bf16[768,256]{1,0:T(8,128)(2,1)S(1)} %get-tuple-element.25), channel_id=1, source_target_pairs={{0,6},{1,7},{2,0},{3,1},{4,2},{5,3},{6,4},{7,5},{8,14},{9,15},{10,... | collective-permute-start | bytes 1179656 | tf_op jit(solution)/shard_map/ppermute | solution.py:52
  96.1 7.7 %collective-permute-done.14.refs_4_ = bf16[768,256]{1,0:T(8,128)(2,1)S(1)} collective-permute-done((bf16[768,256]{1,0:T(8,128)(2,1)S(1)}, bf16[768,256]{1,0:T(8,128)(2,1)S(1)}, u32[]{:S(2)}, u32[]{:S(2)}) %collective-permute-start.14) | collective-permute-done | bytes 393248 | tf_op jit(solution)/shard_map/ppermute | solution.py:52
  103.8 3.2 %early_down.1 = bf16[1536,256]{1,0:T(8,128)(2,1)S(1)} custom-call(s32[3]{0:T(128)S(1)} %pad_add_fusion.place_ref, bf16[2560,1024]{1,0:T(8,128)(2,1)S(1)} %copy-done, bf16[2560,1024]{1,0:T(8,128)(2,1)S(1)} %copy-done, bf16[2,8,64,512]{3,2,1,0:T(8,128)(2,1)S(1)} %bitcast.24, bf16[2,8,64,512]{3,2,1,0:T(8,128)(2,1)S(1)} %bitcast.25, ...), custom_call_target="tpu_custom_call" | custom-call | flops 805306368 | bytes 3932160 | tf_op jit(solution)/shard_map/early_down/pallas_call | solution.py:242
  107.0 3.5 %collective-permute-start.15 = (bf16[1536,256]{1,0:T(8,128)(2,1)S(1)}, bf16[1536,256]{1,0:T(8,128)(2,1)S(1)}, u32[]{:S(2)}, u32[]{:S(2)}) collective-permute-start(bf16[1536,256]{1,0:T(8,128)(2,1)S(1)} %early_down.1), channel_id=1, source_target_pairs={{0,6},{1,7},{2,0},{3,1},{4,2},{5,3},{6,4},{7,5},{8,14},{9,15},{10,... | collective-permute-start | bytes 2359304 | tf_op jit(solution)/shard_map/ppermute | solution.py:52
  110.5 3.2 %early_up.1 = bf16[1536,256]{1,0:T(8,128)(2,1)S(1)} custom-call(s32[3]{0:T(128)S(1)} %pad_add_fusion.place_ref, bf16[2560,1024]{1,0:T(8,128)(2,1)S(1)} %copy-done, bf16[2560,1024]{1,0:T(8,128)(2,1)S(1)} %copy-done, bf16[2,8,64,512]{3,2,1,0:T(8,128)(2,1)S(1)} %bitcast.26, bf16[2,8,64,512]{3,2,1,0:T(8,128)(2,1)S(1)} %bitcast.27, ...), custom_call_target="tpu_custom_call" | custom-call | flops 805306368 | bytes 3932160 | tf_op jit(solution)/shard_map/early_up/pallas_call | solution.py:242
  113.8 2.2 %late_far.1 = bf16[1024,128]{1,0:T(8,128)(2,1)S(1)} custom-call(s32[3]{0:T(128)S(1)} %pad_add_fusion.place_ref, bf16[2560,1024]{1,0:T(8,128)(2,1)S(1)} %copy-done, bf16[2560,1024]{1,0:T(8,128)(2,1)S(1)} %copy-done, bf16[2,8,64,512]{3,2,1,0:T(8,128)(2,1)S(1)} %bitcast.28, bf16[2,8,64,512]{3,2,1,0:T(8,128)(2,1)S(1)} %bitcast.44, ...), custom_call_target="tpu_custom_call" | custom-call | flops 268435456 | bytes 2359296 | tf_op jit(solution)/shard_map/late_far/pallas_call | solution.py:242
  116.0 2.7 %collective-permute-start.20 = (bf16[512,128]{1,0:T(8,128)(2,1)S(1)}, bf16[512,128]{1,0:T(8,128)(2,1)S(1)}, u32[]{:S(2)}, u32[]{:S(2)}) collective-permute-start(bf16[512,128]{1,0:T(8,128)(2,1)S(1)} %get-tuple-element.27), channel_id=1, source_target_pairs={{0,6},{1,7},{2,0},{3,1},{4,2},{5,3},{6,4},{7,5},{8,14},{9,15},{10,... | collective-permute-start | bytes 393224 | tf_op jit(solution)/shard_map/ppermute | solution.py:52
  118.8 6.9 %collective-permute-done.15.refs_3_ = bf16[1536,256]{1,0:T(8,128)(2,1)S(1)} collective-permute-done((bf16[1536,256]{1,0:T(8,128)(2,1)S(1)}, bf16[1536,256]{1,0:T(8,128)(2,1)S(1)}, u32[]{:S(2)}, u32[]{:S(2)}) %collective-permute-start.15) | collective-permute-done | bytes 786464 | tf_op jit(solution)/shard_map/ppermute | solution.py:52
  125.7 6.4 %collective-permute-done.13.refs_2_ = bf16[1536,256]{1,0:T(8,128)(2,1)S(1)} collective-permute-done((bf16[1536,256]{1,0:T(8,128)(2,1)S(1)}, bf16[1536,256]{1,0:T(8,128)(2,1)S(1)}, u32[]{:S(2)}, u32[]{:S(2)}) %collective-permute-start.13) | collective-permute-done | bytes 786464 | tf_op jit(solution)/shard_map/ppermute | solution.py:52
  132.1 3.0 %early_give.1 = bf16[1536,128]{1,0:T(8,128)(2,1)S(1)} custom-call(s32[3]{0:T(128)S(1)} %pad_add_fusion.place_ref, bf16[2560,1024]{1,0:T(8,128)(2,1)S(1)} %copy-done, bf16[2560,1024]{1,0:T(8,128)(2,1)S(1)} %copy-done, bf16[2,8,64,512]{3,2,1,0:T(8,128)(2,1)S(1)} %bitcast.29, bf16[2,8,64,512]{3,2,1,0:T(8,128)(2,1)S(1)} %bitcast.45, ...), custom_call_target="tpu_custom_call" | custom-call | flops 402653184 | bytes 3538944 | tf_op jit(solution)/shard_map/early_give/pallas_call | solution.py:242
  135.9 2.2 %late_down.1 = bf16[1024,128]{1,0:T(8,128)(2,1)S(1)} custom-call(s32[3]{0:T(128)S(1)} %pad_add_fusion.place_ref, bf16[2560,1024]{1,0:T(8,128)(2,1)S(1)} %copy-done, bf16[2560,1024]{1,0:T(8,128)(2,1)S(1)} %copy-done, bf16[2,8,64,512]{3,2,1,0:T(8,128)(2,1)S(1)} %bitcast.30, bf16[2,8,64,512]{3,2,1,0:T(8,128)(2,1)S(1)} %bitcast.46, ...), custom_call_target="tpu_custom_call" | custom-call | flops 268435456 | bytes 2359296 | tf_op jit(solution)/shard_map/late_down/pallas_call | solution.py:242
  138.2 2.2 %late_up.1 = bf16[1024,128]{1,0:T(8,128)(2,1)S(1)} custom-call(s32[3]{0:T(128)S(1)} %pad_add_fusion.place_ref, bf16[2560,1024]{1,0:T(8,128)(2,1)S(1)} %copy-done, bf16[2560,1024]{1,0:T(8,128)(2,1)S(1)} %copy-done, bf16[2,8,64,512]{3,2,1,0:T(8,128)(2,1)S(1)} %bitcast.31, bf16[2,8,64,512]{3,2,1,0:T(8,128)(2,1)S(1)} %bitcast.47, ...), custom_call_target="tpu_custom_call" | custom-call | flops 268435456 | bytes 2359296 | tf_op jit(solution)/shard_map/late_up/pallas_call | solution.py:242
  143.4 3.8 %collective-permute-done.19.refs_3_ = bf16[1024,128]{1,0:T(8,128)(2,1)S(1)} collective-permute-done((bf16[1024,128]{1,0:T(8,128)(2,1)S(1)}, bf16[1024,128]{1,0:T(8,128)(2,1)S(1)}, u32[]{:S(2)}, u32[]{:S(2)}) %collective-permute-start.19) | collective-permute-done | bytes 262176 | tf_op jit(solution)/shard_map/ppermute | solution.py:52
  147.2 2.2 %late_sum.1 = bf16[1024,128]{1,0:T(8,128)(2,1)S(1)} custom-call(s32[3]{0:T(128)S(1)} %pad_add_fusion.place_ref, bf16[2560,1024]{1,0:T(8,128)(2,1)S(1)} %copy-done, bf16[2560,1024]{1,0:T(8,128)(2,1)S(1)} %copy-done, bf16[2,8,64,512]{3,2,1,0:T(8,128)(2,1)S(1)} %bitcast.32, bf16[2,8,64,512]{3,2,1,0:T(8,128)(2,1)S(1)} %bitcast.48, ...), custom_call_target="tpu_custom_call" | custom-call | flops 268435456 | bytes 2359296 | tf_op jit(solution)/shard_map/late_sum/pallas_call | solution.py:242
  149.4 3.0 %early_sum.1 = bf16[1536,128]{1,0:T(8,128)(2,1)S(1)} custom-call(s32[3]{0:T(128)S(1)} %pad_add_fusion.place_ref, bf16[2560,1024]{1,0:T(8,128)(2,1)S(1)} %copy-done, bf16[2560,1024]{1,0:T(8,128)(2,1)S(1)} %copy-done, bf16[2,8,64,512]{3,2,1,0:T(8,128)(2,1)S(1)} %bitcast.33, bf16[2,8,64,512]{3,2,1,0:T(8,128)(2,1)S(1)} %bitcast.49, ...), custom_call_target="tpu_custom_call" | custom-call | flops 402653184 | bytes 3538944 | tf_op jit(solution)/shard_map/early_sum/pallas_call | solution.py:242
  152.5 5.2 %collective-permute-start.22 = (bf16[2560,128]{1,0:T(8,128)(2,1)S(1)}, bf16[2560,128]{1,0:T(8,128)(2,1)S(1)}, u32[]{:S(2)}, u32[]{:S(2)}) collective-permute-start(bf16[2560,128]{1,0:T(8,128)(2,1)S(1)} %pad_maximum_fusion.1.own_ref), channel_id=1, source_target_pairs={{0,8},{8,0},{16,24},{24,16},{32,40},{40,32},{48,56},{56,48},{64,72... | collective-permute-start | bytes 1966088 | tf_op jit(solution)/shard_map/ppermute | solution.py:48
  157.7 1.7 collective-permute-done.22.got_ref
  160.3 6.8 %finish.1 = bf16[64,5120]{1,0:T(8,128)(2,1)} custom-call(s32[3]{0:T(128)} %copy-done.1, bf16[2560,128]{1,0:T(8,128)(2,1)} %copy-done.3, bf16[2560,128]{1,0:T(8,128)(2,1)} %copy-done.4), custom_call_target="tpu_custom_call" | custom-call | tf_op jit(solution)/shard_map/finish/pallas_call | solution.py:274
  (64 shorter events, 17.0 us)
Async XLA Ops:
  6.5 3.6 %copy-start.6 = (bf16[1,512,128]{2,1,0:T(8,128)(2,1)S(1)}, bf16[1,512,128]{2,1,0:T(8,128)(2,1)}, u32[]{:S(2)}) copy-start(bf16[1,512,128]{2,1,0:T(8,128)(2,1)} %param.8) | copy-start | bytes 393220
  6.5 3.6 %copy-start.5 = (bf16[1,512,128]{2,1,0:T(8,128)(2,1)S(1)}, bf16[1,512,128]{2,1,0:T(8,128)(2,1)}, u32[]{:S(2)}) copy-start(bf16[1,512,128]{2,1,0:T(8,128)(2,1)} %param.9) | copy-start | bytes 393220
  6.5 3.7 %copy-start.7 = (bf16[256,128]{1,0:T(8,128)(2,1)S(1)}, bf16[256,128]{1,0:T(8,128)(2,1)}, u32[]{:S(2)}) copy-start(bf16[256,128]{1,0:T(8,128)(2,1)} %param.10) | copy-start | bytes 196612
  6.5 3.7 %copy-start.8 = (bf16[256,128]{1,0:T(8,128)(2,1)S(1)}, bf16[256,128]{1,0:T(8,128)(2,1)}, u32[]{:S(2)}) copy-start(bf16[256,128]{1,0:T(8,128)(2,1)} %param.11) | copy-start | bytes 196612
  6.5 6.3 %copy-start.9 = (s32[16]{0:T(128)S(1)}, s32[16]{0:T(128)}, u32[]{:S(2)}) copy-start(s32[16]{0:T(128)} %param.12) | copy-start | bytes 196
  6.5 74.9 %all-gather.2.cloned.1.call-start = ((), (), s32[]{:S(2)}) async-start(), calls=%async_computation | async-start | bytes 5898240 | tf_op jit(solution)/shard_map/all_gather | solution.py:301
  8.6 13.4 %collective-permute-start = (bf16[512,512]{1,0:T(8,128)(2,1)S(1)}, bf16[512,512]{1,0:T(8,128)(2,1)S(1)}, u32[]{:S(2)}, u32[]{:S(2)}) collective-permute-start(bf16[512,512]{1,0:T(8,128)(2,1)S(1)} %get-tuple-element.24), channel_id=1, source_target_pairs={{0,8},{8,0},{16,24},{24,16},{32,40},{40,32},{48,56},{56,48},{64,72... | collective-permute-start | bytes 1572872 | tf_op jit(solution)/shard_map/ppermute | solution.py:48
  10.1 9.8 %collective-permute-start.6 = (bf16[512,256]{1,0:T(8,128)(2,1)S(1)}, bf16[512,256]{1,0:T(8,128)(2,1)S(1)}, u32[]{:S(2)}, u32[]{:S(2)}) collective-permute-start(bf16[512,256]{1,0:T(8,128)(2,1)S(1)} %get-tuple-element.30), channel_id=1, source_target_pairs={{0,8},{8,0},{16,24},{24,16},{32,40},{40,32},{48,56},{56,48},{64,72... | collective-permute-start | bytes 786440 | tf_op jit(solution)/shard_map/ppermute | solution.py:48
  10.3 5.2 %collective-permute-start.1 = (bf16[256,256]{1,0:T(8,128)(2,1)S(1)}, bf16[256,256]{1,0:T(8,128)(2,1)S(1)}, u32[]{:S(2)}, u32[]{:S(2)}) collective-permute-start(bf16[256,256]{1,0:T(8,128)(2,1)S(1)} %constant_dynamic-update-slice_fusion), channel_id=1, source_target_pairs={{0,64},{8,72},{16,80},{24,88},{32,96},{40,104},{48,112},{56,120},{... | collective-permute-start | bytes 393224 | tf_op jit(solution)/shard_map/ppermute | solution.py:48
  12.1 3.4 %collective-permute-start.7 = (bf16[256,256]{1,0:T(8,128)(2,1)S(1)}, bf16[256,256]{1,0:T(8,128)(2,1)S(1)}, u32[]{:S(2)}, u32[]{:S(2)}) collective-permute-start(bf16[256,256]{1,0:T(8,128)(2,1)S(1)} %constant_dynamic-update-slice_fusion), channel_id=1, source_target_pairs={{0,8},{8,0},{16,24},{24,16},{32,40},{40,32},{48,56},{56,48},{64,72... | collective-permute-start | bytes 393224 | tf_op jit(solution)/shard_map/ppermute | solution.py:48
  15.6 14.2 %collective-permute-start.3 = (bf16[2,256,256]{2,1,0:T(8,128)(2,1)S(1)}, bf16[2,256,256]{2,1,0:T(8,128)(2,1)S(1)}, u32[]{:S(2)}, u32[]{:S(2)}) collective-permute-start(bf16[2,256,256]{2,1,0:T(8,128)(2,1)S(1)} %get-tuple-element.32), channel_id=1, source_target_pairs={{0,16},{8,24},{16,32},{24,40},{32,48},{40,56},{48,0},{56,8},{64,80... | collective-permute-start | bytes 786440 | tf_op jit(solution)/shard_map/ppermute | solution.py:48
  16.8 12.9 %collective-permute-start.4 = (bf16[2,256,256]{2,1,0:T(8,128)(2,1)S(1)}, bf16[2,256,256]{2,1,0:T(8,128)(2,1)S(1)}, u32[]{:S(2)}, u32[]{:S(2)}) collective-permute-start(bf16[2,256,256]{2,1,0:T(8,128)(2,1)S(1)} %get-tuple-element.32), channel_id=1, source_target_pairs={{0,48},{8,56},{16,0},{24,8},{32,16},{40,24},{48,32},{56,40},{64,11... | collective-permute-start | bytes 786440 | tf_op jit(solution)/shard_map/ppermute | solution.py:48
  18.4 17.7 %collective-permute-start.5 = (bf16[2,256,256]{2,1,0:T(8,128)(2,1)S(1)}, bf16[2,256,256]{2,1,0:T(8,128)(2,1)S(1)}, u32[]{:S(2)}, u32[]{:S(2)}) collective-permute-start(bf16[2,256,256]{2,1,0:T(8,128)(2,1)S(1)} %get-tuple-element.32), channel_id=1, source_target_pairs={{0,32},{8,40},{16,48},{24,56},{32,0},{40,8},{48,16},{56,24},{64,96... | collective-permute-start | bytes 786440 | tf_op jit(solution)/shard_map/ppermute | solution.py:48
  19.9 35.5 %collective-permute-start.2 = (bf16[1,256,256]{2,1,0:T(8,128)(2,1)S(1)}, bf16[1,256,256]{2,1,0:T(8,128)(2,1)S(1)}, u32[]{:S(2)}, u32[]{:S(2)}) collective-permute-start(bf16[1,256,256]{2,1,0:T(8,128)(2,1)S(1)} %bitcast.51), channel_id=1, source_target_pairs={{0,8},{8,0},{16,24},{24,16},{32,40},{40,32},{48,56},{56,48},{64,72... | collective-permute-start | bytes 393224 | tf_op jit(solution)/shard_map/ppermute | solution.py:48
  36.0 19.5 %collective-permute-start.10 = (bf16[2,256,256]{2,1,0:T(8,128)(2,1)S(1)}, bf16[2,256,256]{2,1,0:T(8,128)(2,1)S(1)}, u32[]{:S(2)}, u32[]{:S(2)}) collective-permute-start(bf16[2,256,256]{2,1,0:T(8,128)(2,1)S(1)} %collective-permute-done.5.refs_3_), channel_id=1, source_target_pairs={{0,8},{8,0},{16,24},{24,16},{32,40},{40,32},{48,56},{56,48},{64,72... | collective-permute-start | bytes 786440 | tf_op jit(solution)/shard_map/ppermute | solution.py:48
  41.2 14.2 %collective-permute-start.8 = (bf16[2,256,256]{2,1,0:T(8,128)(2,1)S(1)}, bf16[2,256,256]{2,1,0:T(8,128)(2,1)S(1)}, u32[]{:S(2)}, u32[]{:S(2)}) collective-permute-start(bf16[2,256,256]{2,1,0:T(8,128)(2,1)S(1)} %collective-permute-done.3.refs_1_), channel_id=1, source_target_pairs={{0,8},{8,0},{16,24},{24,16},{32,40},{40,32},{48,56},{56,48},{64,72... | collective-permute-start | bytes 786440 | tf_op jit(solution)/shard_map/ppermute | solution.py:48
  41.3 14.3 %collective-permute-start.9 = (bf16[2,256,256]{2,1,0:T(8,128)(2,1)S(1)}, bf16[2,256,256]{2,1,0:T(8,128)(2,1)S(1)}, u32[]{:S(2)}, u32[]{:S(2)}) collective-permute-start(bf16[2,256,256]{2,1,0:T(8,128)(2,1)S(1)} %collective-permute-done.4.refs_2_), channel_id=1, source_target_pairs={{0,8},{8,0},{16,24},{24,16},{32,40},{40,32},{48,56},{56,48},{64,72... | collective-permute-start | bytes 786440 | tf_op jit(solution)/shard_map/ppermute | solution.py:48
  67.9 2.7 %collective-permute-start.11 = (bf16[2,512,512]{2,1,0:T(8,128)(2,1)S(1)}, bf16[2,512,512]{2,1,0:T(8,128)(2,1)S(1)}, u32[]{:S(2)}, u32[]{:S(2)}) collective-permute-start(bf16[2,512,512]{2,1,0:T(8,128)(2,1)S(1)} %attend_last.1), channel_id=1, source_target_pairs={{0,8},{8,0},{16,24},{24,16},{32,40},{40,32},{48,56},{56,48},{64,72... | collective-permute-start | bytes 3145736 | tf_op jit(solution)/shard_map/ppermute | solution.py:48
  68.1 81.3 %copy-start.1 = (s32[3]{0:T(128)}, s32[3]{0:T(128)S(1)}, u32[]{:S(2)}) copy-start(s32[3]{0:T(128)S(1)} %pad_add_fusion.place_ref) | copy-start | bytes 40
  81.5 2.5 %copy-start = (bf16[2560,1024]{1,0:T(8,128)(2,1)S(1)}, bf16[2560,1024]{1,0:T(8,128)(2,1)}, u32[]{:S(2)}) copy-start(bf16[2560,1024]{1,0:T(8,128)(2,1)} %all-gather.2.cloned.1.call-done.w_own_ref.w_other_ref) | copy-start | bytes 15728644
  87.0 26.8 %collective-permute-start.17 = (bf16[1024,512]{1,0:T(8,128)(2,1)S(1)}, bf16[1024,512]{1,0:T(8,128)(2,1)S(1)}, u32[]{:S(2)}, u32[]{:S(2)}) collective-permute-start(bf16[1024,512]{1,0:T(8,128)(2,1)S(1)} %late_give.1), channel_id=1, source_target_pairs={{0,1},{1,0},{2,3},{3,2},{4,5},{5,4},{6,7},{7,6},{8,9},{9,8},{10,11... | collective-permute-start | bytes 3145736 | tf_op jit(solution)/shard_map/ppermute | solution.py:52
  93.5 10.3 %collective-permute-start.14 = (bf16[768,256]{1,0:T(8,128)(2,1)S(1)}, bf16[768,256]{1,0:T(8,128)(2,1)S(1)}, u32[]{:S(2)}, u32[]{:S(2)}) collective-permute-start(bf16[768,256]{1,0:T(8,128)(2,1)S(1)} %get-tuple-element.25), channel_id=1, source_target_pairs={{0,6},{1,7},{2,0},{3,1},{4,2},{5,3},{6,4},{7,5},{8,14},{9,15},{10,... | collective-permute-start | bytes 1179656 | tf_op jit(solution)/shard_map/ppermute | solution.py:52
  96.1 14.4 %collective-permute-start.12 = (bf16[768,256]{1,0:T(8,128)(2,1)S(1)}, bf16[768,256]{1,0:T(8,128)(2,1)S(1)}, u32[]{:S(2)}, u32[]{:S(2)}) collective-permute-start(bf16[768,256]{1,0:T(8,128)(2,1)S(1)} %get-tuple-element.26), channel_id=1, source_target_pairs={{0,2},{1,3},{2,4},{3,5},{4,6},{5,7},{6,0},{7,1},{8,10},{9,11},{10,... | collective-permute-start | bytes 1179656 | tf_op jit(solution)/shard_map/ppermute | solution.py:52
  107.0 18.7 %collective-permute-start.15 = (bf16[1536,256]{1,0:T(8,128)(2,1)S(1)}, bf16[1536,256]{1,0:T(8,128)(2,1)S(1)}, u32[]{:S(2)}, u32[]{:S(2)}) collective-permute-start(bf16[1536,256]{1,0:T(8,128)(2,1)S(1)} %early_down.1), channel_id=1, source_target_pairs={{0,6},{1,7},{2,0},{3,1},{4,2},{5,3},{6,4},{7,5},{8,14},{9,15},{10,... | collective-permute-start | bytes 2359304 | tf_op jit(solution)/shard_map/ppermute | solution.py:52
  113.7 18.4 %collective-permute-start.13 = (bf16[1536,256]{1,0:T(8,128)(2,1)S(1)}, bf16[1536,256]{1,0:T(8,128)(2,1)S(1)}, u32[]{:S(2)}, u32[]{:S(2)}) collective-permute-start(bf16[1536,256]{1,0:T(8,128)(2,1)S(1)} %early_up.1), channel_id=1, source_target_pairs={{0,2},{1,3},{2,4},{3,5},{4,6},{5,7},{6,0},{7,1},{8,10},{9,11},{10,... | collective-permute-start | bytes 2359304 | tf_op jit(solution)/shard_map/ppermute | solution.py:52
  116.0 19.9 %collective-permute-start.20 = (bf16[512,128]{1,0:T(8,128)(2,1)S(1)}, bf16[512,128]{1,0:T(8,128)(2,1)S(1)}, u32[]{:S(2)}, u32[]{:S(2)}) collective-permute-start(bf16[512,128]{1,0:T(8,128)(2,1)S(1)} %get-tuple-element.27), channel_id=1, source_target_pairs={{0,6},{1,7},{2,0},{3,1},{4,2},{5,3},{6,4},{7,5},{8,14},{9,15},{10,... | collective-permute-start | bytes 393224 | tf_op jit(solution)/shard_map/ppermute | solution.py:52
  118.8 19.4 %collective-permute-start.18 = (bf16[512,128]{1,0:T(8,128)(2,1)S(1)}, bf16[512,128]{1,0:T(8,128)(2,1)S(1)}, u32[]{:S(2)}, u32[]{:S(2)}) collective-permute-start(bf16[512,128]{1,0:T(8,128)(2,1)S(1)} %get-tuple-element.28), channel_id=1, source_target_pairs={{0,2},{1,3},{2,4},{3,5},{4,6},{5,7},{6,0},{7,1},{8,10},{9,11},{10,... | collective-permute-start | bytes 393224 | tf_op jit(solution)/shard_map/ppermute | solution.py:52
  135.2 14.2 %collective-permute-start.16 = (bf16[1536,128]{1,0:T(8,128)(2,1)S(1)}, bf16[1536,128]{1,0:T(8,128)(2,1)S(1)}, u32[]{:S(2)}, u32[]{:S(2)}) collective-permute-start(bf16[1536,128]{1,0:T(8,128)(2,1)S(1)} %early_give.1), channel_id=1, source_target_pairs={{0,1},{1,0},{2,3},{3,2},{4,5},{5,4},{6,7},{7,6},{8,9},{9,8},{10,11... | collective-permute-start | bytes 1179656 | tf_op jit(solution)/shard_map/ppermute | solution.py:52
  138.1 5.3 %collective-permute-start.21 = (bf16[1024,128]{1,0:T(8,128)(2,1)S(1)}, bf16[1024,128]{1,0:T(8,128)(2,1)S(1)}, u32[]{:S(2)}, u32[]{:S(2)}) collective-permute-start(bf16[1024,128]{1,0:T(8,128)(2,1)S(1)} %late_down.1), channel_id=1, source_target_pairs={{0,6},{1,7},{2,0},{3,1},{4,2},{5,3},{6,4},{7,5},{8,14},{9,15},{10,... | collective-permute-start | bytes 786440 | tf_op jit(solution)/shard_map/ppermute | solution.py:52
  140.4 6.8 %collective-permute-start.19 = (bf16[1024,128]{1,0:T(8,128)(2,1)S(1)}, bf16[1024,128]{1,0:T(8,128)(2,1)S(1)}, u32[]{:S(2)}, u32[]{:S(2)}) collective-permute-start(bf16[1024,128]{1,0:T(8,128)(2,1)S(1)} %late_up.1), channel_id=1, source_target_pairs={{0,2},{1,3},{2,4},{3,5},{4,6},{5,7},{6,0},{7,1},{8,10},{9,11},{10,... | collective-permute-start | bytes 786440 | tf_op jit(solution)/shard_map/ppermute | solution.py:52
  152.5 6.9 %copy-start.3 = (bf16[2560,128]{1,0:T(8,128)(2,1)}, bf16[2560,128]{1,0:T(8,128)(2,1)S(1)}, u32[]{:S(2)}) copy-start(bf16[2560,128]{1,0:T(8,128)(2,1)S(1)} %pad_maximum_fusion.1.own_ref) | copy-start | bytes 1966084
  152.5 6.9 %collective-permute-start.22 = (bf16[2560,128]{1,0:T(8,128)(2,1)S(1)}, bf16[2560,128]{1,0:T(8,128)(2,1)S(1)}, u32[]{:S(2)}, u32[]{:S(2)}) collective-permute-start(bf16[2560,128]{1,0:T(8,128)(2,1)S(1)} %pad_maximum_fusion.1.own_ref), channel_id=1, source_target_pairs={{0,8},{8,0},{16,24},{24,16},{32,40},{40,32},{48,56},{56,48},{64,72... | collective-permute-start | bytes 1966088 | tf_op jit(solution)/shard_map/ppermute | solution.py:48
  (2 other events, 2.2 us)
Sparse Core Ops, SparseCore 0:
  9.0 72.3 all-gather.1

commit v2 on v1

v2 whole, which is shorter than its diff:
```python
import functools
import math

import jax
import jax.numpy as jnp
from jax import lax
from jax.experimental import pallas as pl
from jax.experimental.pallas import tpu as pltpu
from jax.sharding import PartitionSpec as P

HD = 128
HEADS = 4
TILE = 256
SCALE = HD ** (-0.5) * math.log2(math.e)
BF = jnp.bfloat16
F32 = jnp.float32
NT = (((1,), (1,)), ((), ()))


def sample_pairs(to):
    place = lambda z, y, c: (z * 4 + y) * 2 + c
    return [
        (place(z, y, c), place(*to(z, y, c)))
        for z in range(2) for y in range(4) for c in range(2)
    ]


def head_pairs(to):
    pairs = []
    for x in range(4):
        for z in range(2):
            tx, tz = to(x, z)
            pairs.append((x * 2 + z, tx * 2 + tz))
    return pairs


CORE = sample_pairs(lambda z, y, c: (z, y, 1 - c))
ZLO = sample_pairs(lambda z, y, c: (1 - z, y, c))
YUP = sample_pairs(lambda z, y, c: (z, (y + 1) % 4, c))
YDOWN = sample_pairs(lambda z, y, c: (z, (y + 3) % 4, c))
YFAR = sample_pairs(lambda z, y, c: (z, (y + 2) % 4, c))
XUP = head_pairs(lambda x, z: ((x + 1) % 4, z))
XDOWN = head_pairs(lambda x, z: ((x + 3) % 4, z))
ZHI = head_pairs(lambda x, z: (x, 1 - z))


def over_sample(value, pairs):
    return lax.ppermute(value, "sample", pairs)


def over_head(value, pairs):
    return lax.ppermute(value, "head", pairs)


X, Z_HI, CORE_AT, Y, Z_LO, LENGTH = range(6)


def attend_kernel(counts, samples, first, last, place_ref, q_own_ref, q_got_ref, *refs):
    refs = list(refs)
    suffix_refs = [refs.pop(0) for _ in range(4)] if first else None
    kv_refs = [refs.pop(0) for _ in counts]
    acc_in, stat_in = (None, None) if first else (refs.pop(0), refs.pop(0))
    if last:
        out_ref = refs.pop(0)
    else:
        acc_out, stat_out = refs.pop(0), refs.pop(0)
    keys_ref, values_ref = refs.pop(0), refs.pop(0)
    step, tile = pl.program_id(0), pl.program_id(1)
    sample = samples[0] + step
    rows_total = keys_ref.shape[0]

    @pl.when((step == 0) & (tile == 0))
    def _():
        at = 0
        for kv_ref, count in zip(kv_refs, counts):
            for b in range(count):
                block = kv_ref[b]
                rows = block.shape[0]
                keys_ref[at:at + rows] = block[:, :HD]
                values_ref[at:at + rows, :HD] = block[:, HD:]
                at += rows
        values_ref[:, HD:] = jnp.ones((rows_total, HD), BF)

    length = place_ref[LENGTH + sample]
    live = tile * TILE < length

    def pick(own, got):
        if len(samples) == 1:
            return got if samples[0] else own
        return jnp.where(sample == 0, own, got)

    def fold(state, scores, values):
        top = jnp.max(scores, axis=1, keepdims=True)
        if state is None:
            weights = jnp.exp2(scores - top)
            return top, jnp.dot(weights.astype(BF), values, preferred_element_type=F32)
        old, acc = state
        top = jnp.maximum(old, top)
        weights = jnp.exp2(scores - top)
        part = jnp.dot(weights.astype(BF), values, preferred_element_type=F32)
        return top, acc * jnp.exp2(old - top) + part

    def body(tile_static):
        for h in range(HEADS):
            cols = slice(h * HD, (h + 1) * HD)
            q = pick(q_own_ref[:, cols].astype(F32), q_got_ref[:, cols].astype(F32))
            q = (q * SCALE).astype(BF)
            state = None
            if first:
                row = lax.broadcasted_iota(jnp.int32, (TILE, TILE), 0)
                col = lax.broadcasted_iota(jnp.int32, (TILE, TILE), 1)
                for t in range(tile_static, -1, -1):
                    lines = slice(t * TILE, (t + 1) * TILE)
                    keys, values = (
                        pick(suffix_refs[i][lines], suffix_refs[i + 2][lines]) for i in (0, 1)
                    )
                    scores = lax.dot_general(q, keys, NT, preferred_element_type=F32)
                    if t == tile_static:
                        scores = jnp.where(col <= row, scores, -1e30)
                    values = jnp.concatenate([values, jnp.ones((TILE, HD), BF)], 1)
                    state = fold(state, scores, values)
            at = 0
            size = TILE if first else rows_total
            while at < rows_total:
                scores = lax.dot_general(q, keys_ref[at:at + size], NT, preferred_element_type=F32)
                state = fold(state, scores, values_ref[at:at + size])
                at += size
            top, acc = state
            num, den = acc[:, :HD], acc[:, HD:]
            if not first:
                top = jnp.broadcast_to(top, (TILE, HD))
                old = jnp.broadcast_to(stat_in[:, h:h + 1], (TILE, HD))
                total = jnp.broadcast_to(stat_in[:, HEADS + h:HEADS + h + 1], (TILE, HD))
                new = jnp.maximum(old, top)
                keep, add = jnp.exp2(old - new), jnp.exp2(top - new)
                num = acc_in[:, cols] * keep + num * add
                den = total * keep + den * add
                top = new[:, :1]
            if last:
                row = tile * TILE + lax.broadcasted_iota(jnp.int32, (TILE, HD), 0)
                out_ref[:, cols] = jnp.where(row < length, num / den, 0.0).astype(BF)
            else:
                acc_out[:, cols] = num
                stat_out[:, h:h + 1] = top
                stat_out[:, HEADS + h:HEADS + h + 1] = den[:, :1]

    if first:
        for t in range(2):
            pl.when(live & (tile == t))(functools.partial(body, t))
    else:
        pl.when(live)(functools.partial(body, 0))

    if last:
        @pl.when(jnp.logical_not(live))
        def _():
            out_ref[...] = jnp.zeros_like(out_ref)


def attend(place, q_own, q_got, suffixes, kvs, state, samples, last, name):
    first = state is None
    rows, width = q_got.shape[0], q_got.shape[1] // 2
    counts = [kv.shape[0] for kv in kvs]
    keys_total = sum(kv.shape[0] * kv.shape[1] for kv in kvs)
    tiled = lambda w, base: pl.BlockSpec((None, TILE, w), lambda s, t, p: (base + s, t, 0))
    whole = lambda a: pl.BlockSpec(a.shape, lambda s, t, p: (0,) * a.ndim)
    in_specs = [
        pl.BlockSpec((TILE, width), lambda s, t, p: (t, p[CORE_AT])),
        pl.BlockSpec((TILE, width), lambda s, t, p: (t, p[CORE_AT])),
    ]
    args = [q_own, q_got]
    for array in ([*suffixes] if first else []) + kvs:
        in_specs.append(whole(array))
        args.append(array)
    if not first:
        in_specs += [tiled(width, samples[0]), tiled(HD, samples[0])]
        args += list(state)
    count = len(samples)
    if last:
        out_specs = tiled(width, 0)
        out_shape = jax.ShapeDtypeStruct((count, rows, width), BF)
    else:
        out_specs = [tiled(width, 0), tiled(HD, 0)]
        out_shape = [
            jax.ShapeDtypeStruct((count, rows, width), F32),
            jax.ShapeDtypeStruct((count, rows, HD), F32),
        ]
    keys_seen = keys_total + (rows // 2 if first else 0)
    return pl.pallas_call(
        functools.partial(attend_kernel, counts, samples, first, last),
        grid_spec=pltpu.PrefetchScalarGridSpec(
            num_scalar_prefetch=1,
            grid=(count, rows // TILE),
            in_specs=in_specs,
            out_specs=out_specs,
            scratch_shapes=[
                pltpu.VMEM((keys_total, HD), BF),
                pltpu.VMEM((keys_total, 2 * HD), BF),
            ],
        ),
        out_shape=out_shape,
        name=name,
        cost_estimate=pl.CostEstimate(
            flops=count * rows * HEADS * keys_seen * HD * 32,
            bytes_accessed=4 * count * 2**20,
            transcendentals=count * rows * HEADS * keys_seen,
        ),
        compiler_params=pltpu.CompilerParams(vmem_limit_bytes=48 * 2**20),
    )(place, *args)


OTHER, OWN = False, True


def project_kernel(tiles, count, spans, place_ref, *refs):
    weight_refs = refs[:2 * tiles]
    rows_refs = refs[2 * tiles:2 * tiles + 4 * count]
    add_refs, out_ref = refs[2 * tiles + 4 * count:-1], refs[-1]
    tile = pl.program_id(0)
    own = jnp.concatenate([r[...] for b in range(count) for r in rows_refs[4 * b:4 * b + 2]], axis=0)
    other = jnp.concatenate(
        [r[...] for b in range(count) for r in rows_refs[4 * b + 2:4 * b + 4]], axis=0
    )

    def body(at):
        acc = lax.dot_general(weight_refs[2 * at][...], own, NT, preferred_element_type=F32)
        acc += lax.dot_general(weight_refs[2 * at + 1][...], other, NT, preferred_element_type=F32)
        for ref, (start, length) in zip(add_refs, spans):
            if start <= at < start + length:
                acc += ref[...].astype(F32)
        out_ref[...] = acc.astype(BF)

    for at in range(tiles):
        pl.when(tile == at)(functools.partial(body, at))


def project(place, weights, rows, blocks, adds, name):
    tiles = len(weights)
    size = weights[0].shape[0]
    part, depth = rows[0].shape[1:]
    lanes = 2 * part * len(blocks)

    def rows_spec(step, own):
        def index(i, p):
            z = p[Z_HI] if own else 1 - p[Z_HI]
            return (2 * lax.rem(p[X] + step, 4) + z, 0, 0)

        return pl.BlockSpec((None, part, depth), index)

    def add_spec(lane, start, count):
        return pl.BlockSpec(
            (size, lanes), lambda i, p: (jnp.clip(i - start, 0, count - 1), lane)
        )

    in_specs, args = [], []
    for weight in weights:
        in_specs.append(pl.BlockSpec((size, depth), lambda i, p: (0, p[CORE_AT])))
        in_specs.append(pl.BlockSpec((size, depth), lambda i, p: (0, 1 - p[CORE_AT])))
        args += [weight, weight]
    for block in blocks:
        in_specs += [rows_spec(*block)] * 4
        args += rows
    for array, lane, start, count in adds:
        in_specs.append(add_spec(lane, start, count))
        args.append(array)
    return pl.pallas_call(
        functools.partial(project_kernel, tiles, len(blocks), [a[2:] for a in adds]),
        grid_spec=pltpu.PrefetchScalarGridSpec(
            num_scalar_prefetch=1,
            grid=(tiles,),
            in_specs=in_specs,
            out_specs=pl.BlockSpec((size, lanes), lambda i, p: (i, 0)),
        ),
        out_shape=jax.ShapeDtypeStruct((tiles * size, lanes), BF),
        name=name,
        cost_estimate=pl.CostEstimate(
            flops=4 * tiles * size * lanes * depth,
            bytes_accessed=4 * tiles * size * depth + 2 * tiles * size * lanes,
            transcendentals=0,
        ),
        compiler_params=pltpu.CompilerParams(vmem_limit_bytes=32 * 2**20),
    )(place, *args)


def sum_over_head(place, weights, rows, tag):
    run = lambda w, blocks, adds, name: project(place, w, rows, blocks, adds, name + tag)
    both = lambda step: [(step, OTHER), (step, OWN)]
    n = len(weights) // 2
    top, low = weights[:n], weights[n:]
    via_up = over_head(run(top, both(2), [], "far_top"), XUP)
    via_down = over_head(run(low, both(2), [], "far_low"), XDOWN)
    below_low = over_head(run(low, both(1), [], "up_low"), XUP)
    above_top = over_head(run(top, both(3), [], "down_top"), XDOWN)
    below_top = over_head(run(top, both(1), [(via_up, 0, 0, n)], "up_top"), XUP)
    last = run(low, both(3), [(via_down, 0, 0, n)], "down_low")
    above_low = over_head(last, XDOWN)

    def arrived(lane):
        return [
            (below_top, lane, 0, n), (above_top, lane, 0, n),
            (below_low, lane, n, n), (above_low, lane, n, n),
        ]

    from_z = over_head(run(weights, [(0, OTHER)], arrived(0), "give"), ZHI)
    return run(weights, [(0, OWN)], arrived(1) + [(from_z, 0, 0, 2 * n)], "sum"), last


SPOTS = ((0, 3, 4, 2), (1, 7, 5, 6))


def finish_kernel(cols, blocks, place_ref, spot_ref, *refs):
    own_refs, got_refs, out_ref = refs[:2], refs[2:4], refs[4]
    lane = lax.broadcasted_iota(jnp.int32, (64, 128), 1)
    row = lax.broadcasted_iota(jnp.int32, (64, 128), 0)
    turn = lambda array, at: lax.dot_general(
        jnp.where(lane == row + at, 1.0, 0.0).astype(BF), array, NT, preferred_element_type=F32
    )
    first = place_ref[CORE_AT] == 0
    count = len(SPOTS) * len(SPOTS[0]) // 2
    for b in range(blocks):
        i = pl.program_id(0) * blocks + b
        dz = lax.rem(i // 4 + place_ref[Z_LO], 2)
        dy = lax.rem(lax.rem(i, 4) + 4 - place_ref[Y], 4)
        spot = spot_ref[dz * 4 + dy]
        lines = pl.ds(pl.multiple_of(lax.rem(spot, count) * cols, cols), cols)
        take = lambda pair: jnp.where(spot < count, pair[0][lines], pair[1][lines])
        own, got = turn(take(own_refs), 0), turn(take(got_refs), 64)
        even, odd = jnp.where(first, own, got), jnp.where(first, got, own)
        out_ref[:, b * 2 * cols:(b + 1) * 2 * cols] = jnp.concatenate([even, odd], axis=1).astype(BF)


def finish(place, own, got, cols):
    spots = jnp.array([s for line in SPOTS for s in line], jnp.int32)
    whole = pl.BlockSpec(own[0].shape, lambda i, p, s: (0, 0))
    blocks = 4
    return pl.pallas_call(
        functools.partial(finish_kernel, cols, blocks),
        grid_spec=pltpu.PrefetchScalarGridSpec(
            num_scalar_prefetch=2,
            grid=(8 // blocks,),
            in_specs=[whole] * 4,
            out_specs=pl.BlockSpec((64, blocks * 2 * cols), lambda i, p, s: (0, i)),
        ),
        out_shape=jax.ShapeDtypeStruct((64, 16 * cols), BF),
        name="finish",
    )(place, spots, *own, *got)


def per_device(
    queries, suffix_keys, suffix_values, prefix_keys, prefix_values, lengths, out_weight
):
    hold = lax.optimization_barrier
    sample = lax.axis_index("sample")
    head = lax.axis_index("head")
    core = sample % 2
    width = queries.shape[2] // 2
    place = jnp.stack([
        head // 2, head % 2, core, (sample // 2) % 4, sample // 8,
        lengths[sample], lengths[sample + 1 - 2 * core],
    ]).astype(jnp.int32)

    kv = jnp.concatenate([prefix_keys, prefix_values], axis=1)
    kv_z = over_sample(kv, ZLO)
    q_own = queries[0]
    q_got = over_sample(q_own, CORE)
    suffix = [suffix_keys[0], suffix_values[0]]
    suffixes = suffix + [over_sample(a, CORE) for a in suffix]
    kv_core = over_sample(kv, CORE)
    near = jnp.stack([kv, kv_z])
    ys = [over_sample(near, to) for to in (YUP, YDOWN, YFAR)]

    w, near = hold((out_weight.T, near))
    w_z = over_sample(w, ZLO)

    run = lambda kvs, state, samples, last, name: attend(
        place, q_own, q_got, suffixes, kvs, state, samples, last, name
    )
    state = run([kv[None], kv_core[None]], None, (0, 1), False, "attend_near")
    ys, state, w_y, wz_y = hold((ys, state, w, w_z))
    w_up, w_down = over_sample(w_y, YUP), over_sample(w_y, YDOWN)
    wz_up, wz_down = over_sample(wz_y, YUP), over_sample(wz_y, YDOWN)
    rest = [jnp.concatenate([kv_z[None]] + ys, axis=0)]
    rest_core = [over_sample(rest[0], CORE)]
    state = run(rest, state, (0, 1), False, "attend_far")
    state, w_up, w_down = hold((state, w_up, w_down))
    half_lines = w.shape[0] // 2
    far_up = over_sample(w_up[:half_lines], YUP)
    far_down = over_sample(w_down[half_lines:], YDOWN)
    own = run(rest_core, state, (0,), True, "attend_own")
    own_core = over_sample(own, CORE)
    state, own = hold((state, own))
    partner = run(rest_core, state, (1,), True, "attend_partner")
    partner_core = over_sample(partner, CORE)
    partner, far_up, far_down = hold((partner, far_up, far_down))
    w_far = jnp.concatenate([far_up, far_down], axis=0)
    wz_far = over_sample(w_far, ZLO)

    rows = [a.reshape(8, 64, width) for a in (own, partner, partner_core, own_core)]
    early, after = sum_over_head(place, [w, w_z, w_up, w_down], rows, "_early")
    w_late, _ = hold(([w_far, wz_far, wz_up, wz_down], after))
    late, _ = sum_over_head(place, w_late, rows, "_late")

    got = [over_sample(early, CORE), over_sample(late, CORE)]
    return finish(place, [early, late], got, out_weight.shape[1])[None]


def solution(mesh):
    placed = (
        P("sample", None, "head"),
        P("sample", None, "head"),
        P("sample", None, "head"),
        P("sample", "head"),
        P("sample", "head"),
        P(),
        P("head", "sample"),
    )
    return jax.shard_map(
        per_device, mesh=mesh, in_specs=placed, out_specs=P("sample", "head", None), check_vma=False
    )
```

time: 174 us -> 156 us (0.90); the launches traced: 174 us -> 154 us
  starting transfers between devices: 36.1 us -> 66.1 us
  waiting for transfers between devices: 49.1 us -> 24.4 us
  Pallas kernels: 66.6 us -> 53.1 us
  between operations: 13.7 us -> 0.52 us
  local copies, waits for them, and re-layouts: 6.75 us -> 9.63 us
    ppermute x10 -> x14, starting transfers between devices: 14.6 us -> 30.2 us  [over_head(): return lax.ppermute(value, 'head', pairs)]
    ppermute x13 -> x21, starting transfers between devices: 21.5 us -> 35.9 us  [over_sample(): return lax.ppermute(value, 'sample', pairs)]
    pallas_call x14 -> x21, Pallas kernels: 66.6 us -> 53.1 us  [the longest x16 29.6 us: project(): pl.pallas_call(functools.partial(project_kernel, tiles, len(blocks), [a[2...]
    ppermute x10 -> x14, waiting for transfers between devices: 26.4 us -> 13.3 us  [over_head(): return lax.ppermute(value, 'head', pairs)]
    all_gather x1 -> x0, waiting for transfers between devices: 10.8 us -> none  [per_device(): lax.all_gather(out_weight.T, 'sample', axis=0, tiled=True, axis_index_gro...]
    unnamed x21 -> x22, local copies, waits for them, and re-layouts: 4.72 us -> 6 us
    ppermute x13 -> x21, waiting for transfers between devices: 11.2 us -> 11.2 us  [over_sample(): return lax.ppermute(value, 'sample', pairs)]
  transfers between devices with their start and end apart: 24 -> 35, of which waited for: 10 -> 12; matrix products, arithmetic and copies ran while one was open for 2% -> 3% of each run, Pallas kernels for 31% -> 32%
where the time goes in v2:
time: 156 us; the launch traced here: 154 us
  starting transfers between devices  66.1 us (42%)
  Pallas kernels  53.1 us (34%)
  waiting for transfers between devices  24.4 us (16%)
  local copies, waits for them, and re-layouts  9.63 us (6%)
    ppermute x21, starting transfers between devices, over_sample(): return lax.ppermute(value, 'sample', pairs)  35.9 us
    ppermute x14, starting transfers between devices, over_head(): return lax.ppermute(value, 'head', pairs)  30.2 us
    pallas_call x16, Pallas kernels, project(): pl.pallas_call(functools.partial(project_kernel, tiles, len(blocks), [a[2...  29.6 us
    pallas_call x4, Pallas kernels, attend(): pl.pallas_call(functools.partial(attend_kernel, counts, samples, first, l...  19.9 us
    ppermute x14, waiting for transfers between devices, over_head(): return lax.ppermute(value, 'head', pairs)  13.3 us
    ppermute x21, waiting for transfers between devices, over_sample(): return lax.ppermute(value, 'sample', pairs)  11.2 us
    unnamed x22, local copies, waits for them, and re-layouts  6 us
    pallas_call x1, Pallas kernels, finish(): pl.pallas_call(functools.partial(finish_kernel, cols, blocks), grid_spec=...  3.58 us
  transfers between devices with their start and end apart: 35, of which 12 were waited for; matrix products, arithmetic and copies ran while one was open for 3% of the time, Pallas kernels for 32%

profile of v2, /device:TPU:1, one launch (start us, length us, event | category | flops | bytes accessed | tf_op | source)
XLA Modules:
  0.0 153.9 jit_solution(4307834851821471251)
XLA Ops:
  3.1 1.8 %collective-permute-start = (bf16[256,256]{1,0:T(8,128)(2,1)S(1)}, bf16[256,256]{1,0:T(8,128)(2,1)S(1)}, u32[]{:S(2)}, u32[]{:S(2)}) collective-permute-start(bf16[256,256]{1,0:T(8,128)(2,1)S(1)} %constant_dynamic-update-slice_fusion), channel_id=1, source_target_pairs={{0,64},{8,72},{16,80},{24,88},{32,96},{40,104},{48,112},{56,120},{... | collective-permute-start | bytes 393224 | tf_op jit(solution)/shard_map/ppermute | solution.py:48
  11.6 1.6 %collective-permute-start.5 = (bf16[2,256,256]{2,1,0:T(8,128)(2,1)S(1)}, bf16[2,256,256]{2,1,0:T(8,128)(2,1)S(1)}, u32[]{:S(2)}, u32[]{:S(2)}) collective-permute-start(bf16[2,256,256]{2,1,0:T(8,128)(2,1)S(1)} %pad_maximum_fusion.1), channel_id=1, source_target_pairs={{0,32},{8,40},{16,48},{24,56},{32,0},{40,8},{48,16},{56,24},{64,96... | collective-permute-start | bytes 786440 | tf_op jit(solution)/shard_map/ppermute | solution.py:48
  17.6 3.5 %attend_near.1 = (f32[2,512,512]{2,1,0:T(8,128)S(1)}, f32[2,512,128]{2,1,0:T(8,128)S(1)}) custom-call(s32[7]{0:T(128)S(1)} %stack.32.place_ref, bf16[512,1024]{1,0:T(8,128)(2,1)S(1)} %bitcast.145, bf16[512,1024]{1,0:T(8,128)(2,1)S(1)} %collective-permute-done.2.q_got_ref, bf16[512,128]{1,0:T(8,128)(2,1)S(1)} %bitcast.150, bf16[512,128]{1,0:T(8,128)(2,1)S(1)} %bitcast.152, ...), custom_call_target="tpu_custom_call" | custom-call | flops 12884901888 | bytes 8388608 | tf_op jit(solution)/shard_map/attend_near/pallas_call | solution.py:188
  22.5 1.6 %collective-permute-done.5 = bf16[2,256,256]{2,1,0:T(8,128)(2,1)S(1)} collective-permute-done((bf16[2,256,256]{2,1,0:T(8,128)(2,1)S(1)}, bf16[2,256,256]{2,1,0:T(8,128)(2,1)S(1)}, u32[]{:S(2)}, u32[]{:S(2)}) %collective-permute-start.5) | collective-permute-done | bytes 262176 | tf_op jit(solution)/shard_map/ppermute | solution.py:48
  24.0 4.1 %collective-permute-done.1.refs_2_.refs_3_ = bf16[320,1024]{1,0:T(8,128)(2,1)S(1)} collective-permute-done((bf16[320,1024]{1,0:T(8,128)(2,1)}, bf16[320,1024]{1,0:T(8,128)(2,1)S(1)}, u32[]{:S(2)}, u32[]{:S(2)}) %collective-permute-start.1) | collective-permute-done | bytes 655392 | tf_op jit(solution)/shard_map/ppermute | solution.py:48
  28.5 2.3 %collective-permute-start.10 = (bf16[320,1024]{1,0:T(8,128)(2,1)S(1)}, bf16[320,1024]{1,0:T(8,128)(2,1)S(1)}, u32[]{:S(2)}, u32[]{:S(2)}) collective-permute-start(bf16[320,1024]{1,0:T(8,128)(2,1)S(1)} %bitcast.131), channel_id=1, source_target_pairs={{0,48},{8,56},{16,0},{24,8},{32,16},{40,24},{48,32},{56,40},{64,11... | collective-permute-start | bytes 1966088 | tf_op jit(solution)/shard_map/ppermute | solution.py:48
  30.9 3.1 %collective-permute-start.11 = (bf16[7,256,256]{2,1,0:T(8,128)(2,1)S(1)}, bf16[7,256,256]{2,1,0:T(8,128)(2,1)S(1)}, u32[]{:S(2)}, u32[]{:S(2)}) collective-permute-start(bf16[7,256,256]{2,1,0:T(8,128)(2,1)S(1)} %pad_maximum_fusion.refs_0_), channel_id=1, source_target_pairs={{0,8},{8,0},{16,24},{24,16},{32,40},{40,32},{48,56},{56,48},{64,72... | collective-permute-start | bytes 2752520 | tf_op jit(solution)/shard_map/ppermute | solution.py:48
  34.0 8.9 %attend_far.1 = (f32[2,512,512]{2,1,0:T(8,128)S(1)}, f32[2,512,128]{2,1,0:T(8,128)S(1)}) custom-call(s32[7]{0:T(128)S(1)} %stack.32.place_ref, bf16[512,1024]{1,0:T(8,128)(2,1)S(1)} %bitcast.146, bf16[512,1024]{1,0:T(8,128)(2,1)S(1)} %collective-permute-done.2.q_got_ref, bf16[7,256,256]{2,1,0:T(8,128)(2,1)S(1)} %pad_maximum_fusion.refs_0_, ...), custom_call_target="tpu_custom_call" | custom-call | flops 30064771072 | bytes 8388608 | tf_op jit(solution)/shard_map/attend_far/pallas_call | solution.py:188
  43.1 4.1 %collective-permute-start.12 = (bf16[160,1024]{1,0:T(8,128)(2,1)S(1)}, bf16[160,1024]{1,0:T(8,128)(2,1)S(1)}, u32[]{:S(2)}, u32[]{:S(2)}) collective-permute-start(bf16[160,1024]{1,0:T(8,128)(2,1)S(1)} %slice.6), channel_id=1, source_target_pairs={{0,16},{8,24},{16,32},{24,40},{32,48},{40,56},{48,0},{56,8},{64,80... | collective-permute-start | bytes 983048 | tf_op jit(solution)/shard_map/ppermute | solution.py:48
  48.1 3.8 %attend_own.1 = bf16[1,512,512]{2,1,0:T(8,128)(2,1)S(1)} custom-call(s32[7]{0:T(128)S(1)} %stack.32.place_ref, bf16[512,1024]{1,0:T(8,128)(2,1)S(1)} %bitcast.147, bf16[512,1024]{1,0:T(8,128)(2,1)S(1)} %collective-permute-done.2.q_got_ref, bf16[7,256,256]{2,1,0:T(8,128)(2,1)S(1)} %collective-permute-done.11.refs_0_, ...), custom_call_target="tpu_custom_call" | custom-call | flops 15032385536 | bytes 4194304 | tf_op jit(solution)/shard_map/attend_own/pallas_call | solution.py:188
  51.9 3.8 %attend_partner.1 = bf16[1,512,512]{2,1,0:T(8,128)(2,1)S(1)} custom-call(s32[7]{0:T(128)S(1)} %stack.32.place_ref, bf16[512,1024]{1,0:T(8,128)(2,1)S(1)} %bitcast.148, bf16[512,1024]{1,0:T(8,128)(2,1)S(1)} %collective-permute-done.2.q_got_ref, bf16[7,256,256]{2,1,0:T(8,128)(2,1)S(1)} %collective-permute-done.11.refs_0_, ...), custom_call_target="tpu_custom_call" | custom-call | flops 15032385536 | bytes 4194304 | tf_op jit(solution)/shard_map/attend_partner/pallas_call | solution.py:188
  55.6 2.2 %collective-permute-start.14 = (bf16[1,512,512]{2,1,0:T(8,128)(2,1)S(1)}, bf16[1,512,512]{2,1,0:T(8,128)(2,1)S(1)}, u32[]{:S(2)}, u32[]{:S(2)}) collective-permute-start(bf16[1,512,512]{2,1,0:T(8,128)(2,1)S(1)} %attend_partner.1), channel_id=1, source_target_pairs={{0,8},{8,0},{16,24},{24,16},{32,40},{40,32},{48,56},{56,48},{64,72... | collective-permute-start | bytes 1572872 | tf_op jit(solution)/shard_map/ppermute | solution.py:48
  57.9 5.2 %collective-permute-start.24 = (bf16[320,1024]{1,0:T(8,128)(2,1)S(1)}, bf16[320,1024]{1,0:T(8,128)(2,1)S(1)}, u32[]{:S(2)}, u32[]{:S(2)}) collective-permute-start(bf16[320,1024]{1,0:T(8,128)(2,1)S(1)} %collective-permute-done.1.refs_2_.refs_3_), channel_id=1, source_target_pairs={{0,16},{8,24},{16,32},{24,40},{32,48},{40,56},{48,0},{56,8},{64,80... | collective-permute-start | bytes 1966088 | tf_op jit(solution)/shard_map/ppermute | solution.py:48
  63.0 2.0 %collective-permute-start.25 = (bf16[320,1024]{1,0:T(8,128)(2,1)S(1)}, bf16[320,1024]{1,0:T(8,128)(2,1)S(1)}, u32[]{:S(2)}, u32[]{:S(2)}) collective-permute-start(bf16[320,1024]{1,0:T(8,128)(2,1)S(1)} %collective-permute-done.1.refs_2_.refs_3_), channel_id=1, source_target_pairs={{0,48},{8,56},{16,0},{24,8},{32,16},{40,24},{48,32},{56,40},{64,11... | collective-permute-start | bytes 1966088 | tf_op jit(solution)/shard_map/ppermute | solution.py:48
  66.8 2.5 %collective-permute-start.20 = (bf16[640,256]{1,0:T(8,128)(2,1)S(1)}, bf16[640,256]{1,0:T(8,128)(2,1)S(1)}, u32[]{:S(2)}, u32[]{:S(2)}) collective-permute-start(bf16[640,256]{1,0:T(8,128)(2,1)S(1)} %far_low_early.1), channel_id=1, source_target_pairs={{0,6},{1,7},{2,0},{3,1},{4,2},{5,3},{6,4},{7,5},{8,14},{9,15},{10,... | collective-permute-start | bytes 983048 | tf_op jit(solution)/shard_map/ppermute | solution.py:52
  72.5 3.0 %collective-permute-done.20.refs_12_ = bf16[640,256]{1,0:T(8,128)(2,1)S(1)} collective-permute-done((bf16[640,256]{1,0:T(8,128)(2,1)S(1)}, bf16[640,256]{1,0:T(8,128)(2,1)S(1)}, u32[]{:S(2)}, u32[]{:S(2)}) %collective-permute-start.20) | collective-permute-done | bytes 327712 | tf_op jit(solution)/shard_map/ppermute | solution.py:52
  77.1 2.7 %collective-permute-done.24.refs_0_.refs_1_.refs_4_.refs_5_ = bf16[320,1024]{1,0:T(8,128)(2,1)S(1)} collective-permute-done((bf16[320,1024]{1,0:T(8,128)(2,1)S(1)}, bf16[320,1024]{1,0:T(8,128)(2,1)S(1)}, u32[]{:S(2)}, u32[]{:S(2)}) %collective-permute-start.24) | collective-permute-done | bytes 655392 | tf_op jit(solution)/shard_map/ppermute | solution.py:48
  82.3 11.1 %collective-permute-start.26 = (bf16[640,256]{1,0:T(8,128)(2,1)S(1)}, bf16[640,256]{1,0:T(8,128)(2,1)S(1)}, u32[]{:S(2)}, u32[]{:S(2)}) collective-permute-start(bf16[640,256]{1,0:T(8,128)(2,1)S(1)} %far_top_late.1), channel_id=1, source_target_pairs={{0,2},{1,3},{2,4},{3,5},{4,6},{5,7},{6,0},{7,1},{8,10},{9,11},{10,... | collective-permute-start | bytes 983048 | tf_op jit(solution)/shard_map/ppermute | solution.py:52
  94.9 1.5 %collective-permute-start.30 = (bf16[640,256]{1,0:T(8,128)(2,1)S(1)}, bf16[640,256]{1,0:T(8,128)(2,1)S(1)}, u32[]{:S(2)}, u32[]{:S(2)}) collective-permute-start(bf16[640,256]{1,0:T(8,128)(2,1)S(1)} %far_low_late.1), channel_id=1, source_target_pairs={{0,6},{1,7},{2,0},{3,1},{4,2},{5,3},{6,4},{7,5},{8,14},{9,15},{10,... | collective-permute-start | bytes 983048 | tf_op jit(solution)/shard_map/ppermute | solution.py:52
  104.3 2.7 %collective-permute-start.21 = (bf16[640,256]{1,0:T(8,128)(2,1)S(1)}, bf16[640,256]{1,0:T(8,128)(2,1)S(1)}, u32[]{:S(2)}, u32[]{:S(2)}) collective-permute-start(bf16[640,256]{1,0:T(8,128)(2,1)S(1)} %down_low_early.1), channel_id=1, source_target_pairs={{0,6},{1,7},{2,0},{3,1},{4,2},{5,3},{6,4},{7,5},{8,14},{9,15},{10,... | collective-permute-start | bytes 983048 | tf_op jit(solution)/shard_map/ppermute | solution.py:52
  111.8 2.6 %collective-permute-done.17.refs_12_ = bf16[640,256]{1,0:T(8,128)(2,1)S(1)} collective-permute-done((bf16[640,256]{1,0:T(8,128)(2,1)S(1)}, bf16[640,256]{1,0:T(8,128)(2,1)S(1)}, u32[]{:S(2)}, u32[]{:S(2)}) %collective-permute-start.17) | collective-permute-done | bytes 327712 | tf_op jit(solution)/shard_map/ppermute | solution.py:52
  114.4 2.3 %collective-permute-start.31 = (bf16[640,256]{1,0:T(8,128)(2,1)S(1)}, bf16[640,256]{1,0:T(8,128)(2,1)S(1)}, u32[]{:S(2)}, u32[]{:S(2)}) collective-permute-start(bf16[640,256]{1,0:T(8,128)(2,1)S(1)} %down_low_late.1), channel_id=1, source_target_pairs={{0,6},{1,7},{2,0},{3,1},{4,2},{5,3},{6,4},{7,5},{8,14},{9,15},{10,... | collective-permute-start | bytes 983048 | tf_op jit(solution)/shard_map/ppermute | solution.py:52
  116.7 2.8 %give_early.1 = bf16[1280,128]{1,0:T(8,128)(2,1)S(1)} custom-call(s32[7]{0:T(128)S(1)} %stack.32.place_ref, bf16[320,1024]{1,0:T(8,128)(2,1)S(1)} %bitcast.138, bf16[320,1024]{1,0:T(8,128)(2,1)S(1)} %bitcast.139, bf16[320,1024]{1,0:T(8,128)(2,1)S(1)} %collective-permute-done.1.refs_2_.refs_3_, bf16[320,1024]{1,0:T(8,128)(2,1)S(1)} %collective-permute-done.1.refs_2_.refs_3_, ...), custom_call_target="tpu_custom_call" | custom-call | flops 335544320 | bytes 2949120 | tf_op jit(solution)/shard_map/give_early/pallas_call | solution.py:265
  119.5 3.3 %collective-permute-start.22 = (bf16[1280,128]{1,0:T(8,128)(2,1)S(1)}, bf16[1280,128]{1,0:T(8,128)(2,1)S(1)}, u32[]{:S(2)}, u32[]{:S(2)}) collective-permute-start(bf16[1280,128]{1,0:T(8,128)(2,1)S(1)} %give_early.1), channel_id=1, source_target_pairs={{0,1},{1,0},{2,3},{3,2},{4,5},{5,4},{6,7},{7,6},{8,9},{9,8},{10,11... | collective-permute-start | bytes 983048 | tf_op jit(solution)/shard_map/ppermute | solution.py:52
  123.4 5.8 %collective-permute-done.27.refs_12_ = bf16[640,256]{1,0:T(8,128)(2,1)S(1)} collective-permute-done((bf16[640,256]{1,0:T(8,128)(2,1)S(1)}, bf16[640,256]{1,0:T(8,128)(2,1)S(1)}, u32[]{:S(2)}, u32[]{:S(2)}) %collective-permute-start.27) | collective-permute-done | bytes 327712 | tf_op jit(solution)/shard_map/ppermute | solution.py:52
  130.4 2.8 %give_late.1 = bf16[1280,128]{1,0:T(8,128)(2,1)S(1)} custom-call(s32[7]{0:T(128)S(1)} %stack.32.place_ref, bf16[320,1024]{1,0:T(8,128)(2,1)S(1)} %constant_dynamic-update-slice_fusion.2.refs_0_.refs_1_, bf16[320,1024]{1,0:T(8,128)(2,1)S(1)} %constant_dynamic-update-slice_fusion.2.refs_0_.refs_1_, ...), custom_call_target="tpu_custom_call" | custom-call | flops 335544320 | bytes 2949120 | tf_op jit(solution)/shard_map/give_late/pallas_call | solution.py:265
  133.2 3.3 %collective-permute-start.32 = (bf16[1280,128]{1,0:T(8,128)(2,1)S(1)}, bf16[1280,128]{1,0:T(8,128)(2,1)S(1)}, u32[]{:S(2)}, u32[]{:S(2)}) collective-permute-start(bf16[1280,128]{1,0:T(8,128)(2,1)S(1)} %give_late.1), channel_id=1, source_target_pairs={{0,1},{1,0},{2,3},{3,2},{4,5},{5,4},{6,7},{7,6},{8,9},{9,8},{10,11... | collective-permute-start | bytes 983048 | tf_op jit(solution)/shard_map/ppermute | solution.py:52
  136.6 2.8 %sum_early.1.refs_0_ = bf16[1280,128]{1,0:T(8,128)(2,1)S(1)} custom-call(s32[7]{0:T(128)S(1)} %stack.32.place_ref, bf16[320,1024]{1,0:T(8,128)(2,1)S(1)} %bitcast.140, bf16[320,1024]{1,0:T(8,128)(2,1)S(1)} %bitcast.141, bf16[320,1024]{1,0:T(8,128)(2,1)S(1)} %collective-permute-done.1.refs_2_.refs_3_, ...), custom_call_target="tpu_custom_call" | custom-call | flops 335544320 | bytes 2949120 | tf_op jit(solution)/shard_map/sum_early/pallas_call | solution.py:265
  139.4 3.1 %collective-permute-start.33 = (bf16[1280,128]{1,0:T(8,128)(2,1)S(1)}, bf16[1280,128]{1,0:T(8,128)(2,1)S(1)}, u32[]{:S(2)}, u32[]{:S(2)}) collective-permute-start(bf16[1280,128]{1,0:T(8,128)(2,1)S(1)} %sum_early.1.refs_0_), channel_id=1, source_target_pairs={{0,8},{8,0},{16,24},{24,16},{32,40},{40,32},{48,56},{56,48},{64,72... | collective-permute-start | bytes 983048 | tf_op jit(solution)/shard_map/ppermute | solution.py:48
  142.5 2.8 %sum_late.1.refs_1_ = bf16[1280,128]{1,0:T(8,128)(2,1)S(1)} custom-call(s32[7]{0:T(128)S(1)} %stack.32.place_ref, bf16[320,1024]{1,0:T(8,128)(2,1)S(1)} %constant_dynamic-update-slice_fusion.2.refs_0_.refs_1_, bf16[320,1024]{1,0:T(8,128)(2,1)S(1)} %constant_dynamic-update-slice_fusion.2.refs_0_.refs_1_, ...), custom_call_target="tpu_custom_call" | custom-call | flops 335544320 | bytes 2949120 | tf_op jit(solution)/shard_map/sum_late/pallas_call | solution.py:265
  145.4 2.8 %collective-permute-start.34 = (bf16[1280,128]{1,0:T(8,128)(2,1)S(1)}, bf16[1280,128]{1,0:T(8,128)(2,1)S(1)}, u32[]{:S(2)}, u32[]{:S(2)}) collective-permute-start(bf16[1280,128]{1,0:T(8,128)(2,1)S(1)} %sum_late.1.refs_1_), channel_id=1, source_target_pairs={{0,8},{8,0},{16,24},{24,16},{32,40},{40,32},{48,56},{56,48},{64,72... | collective-permute-start | bytes 983048 | tf_op jit(solution)/shard_map/ppermute | solution.py:48
  150.1 3.6 %finish.1 = bf16[64,5120]{1,0:T(8,128)(2,1)} custom-call(s32[7]{0:T(128)} %copy-done.3, s32[8]{0:T(128)} %constant.70.clone.spot_ref, bf16[1280,128]{1,0:T(8,128)(2,1)} %copy-done.1, bf16[1280,128]{1,0:T(8,128)(2,1)} %copy-done.2, bf16[1280,128]{1,0:T(8,128)(2,1)} %copy-done.8, bf16[1280,128]{1,0:T(8,128)(2,1)} %copy-done.9), custom_call_target="tpu_custom_call" | custom-call | tf_op jit(solution)/shard_map/finish/pallas_call | solution.py:335
  (89 shorter events, 44.1 us)
Async XLA Ops:
  0.0 14.6 %collective-permute-start.2 = (bf16[512,1024]{1,0:T(8,128)(2,1)}, bf16[512,1024]{1,0:T(8,128)(2,1)S(1)}, u32[]{:S(2)}, u32[]{:S(2)}) collective-permute-start(bf16[512,1024]{1,0:T(8,128)(2,1)} %bitcast.144), channel_id=1, source_target_pairs={{0,8},{8,0},{16,24},{24,16},{32,40},{40,32},{48,56},{56,48},{64,72... | collective-permute-start | bytes 3145736 | tf_op jit(solution)/shard_map/ppermute | solution.py:48
  5.2 6.4 %collective-permute-start.7 = (bf16[512,128]{1,0:T(8,128)(2,1)}, bf16[512,128]{1,0:T(8,128)(2,1)S(1)}, u32[]{:S(2)}, u32[]{:S(2)}) collective-permute-start(bf16[512,128]{1,0:T(8,128)(2,1)} %bitcast.151), channel_id=1, source_target_pairs={{0,8},{8,0},{16,24},{24,16},{32,40},{40,32},{48,56},{56,48},{64,72... | collective-permute-start | bytes 393224 | tf_op jit(solution)/shard_map/ppermute | solution.py:48
  5.5 7.7 %collective-permute-start.8 = (bf16[256,256]{1,0:T(8,128)(2,1)S(1)}, bf16[256,256]{1,0:T(8,128)(2,1)S(1)}, u32[]{:S(2)}, u32[]{:S(2)}) collective-permute-start(bf16[256,256]{1,0:T(8,128)(2,1)S(1)} %constant_dynamic-update-slice_fusion), channel_id=1, source_target_pairs={{0,8},{8,0},{16,24},{24,16},{32,40},{40,32},{48,56},{56,48},{64,72... | collective-permute-start | bytes 393224 | tf_op jit(solution)/shard_map/ppermute | solution.py:48
  8.8 13.6 %collective-permute-start.3 = (bf16[2,256,256]{2,1,0:T(8,128)(2,1)S(1)}, bf16[2,256,256]{2,1,0:T(8,128)(2,1)S(1)}, u32[]{:S(2)}, u32[]{:S(2)}) collective-permute-start(bf16[2,256,256]{2,1,0:T(8,128)(2,1)S(1)} %pad_maximum_fusion.1), channel_id=1, source_target_pairs={{0,16},{8,24},{16,32},{24,40},{32,48},{40,56},{48,0},{56,8},{64,80... | collective-permute-start | bytes 786440 | tf_op jit(solution)/shard_map/ppermute | solution.py:48
  10.1 12.4 %collective-permute-start.4 = (bf16[2,256,256]{2,1,0:T(8,128)(2,1)S(1)}, bf16[2,256,256]{2,1,0:T(8,128)(2,1)S(1)}, u32[]{:S(2)}, u32[]{:S(2)}) collective-permute-start(bf16[2,256,256]{2,1,0:T(8,128)(2,1)S(1)} %pad_maximum_fusion.1), channel_id=1, source_target_pairs={{0,48},{8,56},{16,0},{24,8},{32,16},{40,24},{48,32},{56,40},{64,11... | collective-permute-start | bytes 786440 | tf_op jit(solution)/shard_map/ppermute | solution.py:48
  11.6 12.4 %collective-permute-start.5 = (bf16[2,256,256]{2,1,0:T(8,128)(2,1)S(1)}, bf16[2,256,256]{2,1,0:T(8,128)(2,1)S(1)}, u32[]{:S(2)}, u32[]{:S(2)}) collective-permute-start(bf16[2,256,256]{2,1,0:T(8,128)(2,1)S(1)} %pad_maximum_fusion.1), channel_id=1, source_target_pairs={{0,32},{8,40},{16,48},{24,56},{32,0},{40,8},{48,16},{56,24},{64,96... | collective-permute-start | bytes 786440 | tf_op jit(solution)/shard_map/ppermute | solution.py:48
  13.2 14.9 %collective-permute-start.1 = (bf16[320,1024]{1,0:T(8,128)(2,1)}, bf16[320,1024]{1,0:T(8,128)(2,1)S(1)}, u32[]{:S(2)}, u32[]{:S(2)}) collective-permute-start(bf16[320,1024]{1,0:T(8,128)(2,1)} %bitcast.129), channel_id=1, source_target_pairs={{0,64},{8,72},{16,80},{24,88},{32,96},{40,104},{48,112},{56,120},{... | collective-permute-start | bytes 1966088 | tf_op jit(solution)/shard_map/ppermute | solution.py:48
  28.1 15.0 %collective-permute-start.9 = (bf16[320,1024]{1,0:T(8,128)(2,1)S(1)}, bf16[320,1024]{1,0:T(8,128)(2,1)S(1)}, u32[]{:S(2)}, u32[]{:S(2)}) collective-permute-start(bf16[320,1024]{1,0:T(8,128)(2,1)S(1)} %bitcast.130), channel_id=1, source_target_pairs={{0,16},{8,24},{16,32},{24,40},{32,48},{40,56},{48,0},{56,8},{64,80... | collective-permute-start | bytes 1966088 | tf_op jit(solution)/shard_map/ppermute | solution.py:48
  28.5 14.6 %collective-permute-start.10 = (bf16[320,1024]{1,0:T(8,128)(2,1)S(1)}, bf16[320,1024]{1,0:T(8,128)(2,1)S(1)}, u32[]{:S(2)}, u32[]{:S(2)}) collective-permute-start(bf16[320,1024]{1,0:T(8,128)(2,1)S(1)} %bitcast.131), channel_id=1, source_target_pairs={{0,48},{8,56},{16,0},{24,8},{32,16},{40,24},{48,32},{56,40},{64,11... | collective-permute-start | bytes 1966088 | tf_op jit(solution)/shard_map/ppermute | solution.py:48
  30.9 17.2 %collective-permute-start.11 = (bf16[7,256,256]{2,1,0:T(8,128)(2,1)S(1)}, bf16[7,256,256]{2,1,0:T(8,128)(2,1)S(1)}, u32[]{:S(2)}, u32[]{:S(2)}) collective-permute-start(bf16[7,256,256]{2,1,0:T(8,128)(2,1)S(1)} %pad_maximum_fusion.refs_0_), channel_id=1, source_target_pairs={{0,8},{8,0},{16,24},{24,16},{32,40},{40,32},{48,56},{56,48},{64,72... | collective-permute-start | bytes 2752520 | tf_op jit(solution)/shard_map/ppermute | solution.py:48
  43.1 19.9 %collective-permute-start.12 = (bf16[160,1024]{1,0:T(8,128)(2,1)S(1)}, bf16[160,1024]{1,0:T(8,128)(2,1)S(1)}, u32[]{:S(2)}, u32[]{:S(2)}) collective-permute-start(bf16[160,1024]{1,0:T(8,128)(2,1)S(1)} %slice.6), channel_id=1, source_target_pairs={{0,16},{8,24},{16,32},{24,40},{32,48},{40,56},{48,0},{56,8},{64,80... | collective-permute-start | bytes 983048 | tf_op jit(solution)/shard_map/ppermute | solution.py:48
  47.2 17.9 %collective-permute-start.13 = (bf16[160,1024]{1,0:T(8,128)(2,1)S(1)}, bf16[160,1024]{1,0:T(8,128)(2,1)S(1)}, u32[]{:S(2)}, u32[]{:S(2)}) collective-permute-start(bf16[160,1024]{1,0:T(8,128)(2,1)S(1)} %slice.7), channel_id=1, source_target_pairs={{0,48},{8,56},{16,0},{24,8},{32,16},{40,24},{48,32},{56,40},{64,11... | collective-permute-start | bytes 983048 | tf_op jit(solution)/shard_map/ppermute | solution.py:48
  55.6 9.6 %collective-permute-start.14 = (bf16[1,512,512]{2,1,0:T(8,128)(2,1)S(1)}, bf16[1,512,512]{2,1,0:T(8,128)(2,1)S(1)}, u32[]{:S(2)}, u32[]{:S(2)}) collective-permute-start(bf16[1,512,512]{2,1,0:T(8,128)(2,1)S(1)} %attend_partner.1), channel_id=1, source_target_pairs={{0,8},{8,0},{16,24},{24,16},{32,40},{40,32},{48,56},{56,48},{64,72... | collective-permute-start | bytes 1572872 | tf_op jit(solution)/shard_map/ppermute | solution.py:48
  57.8 7.5 %collective-permute-start.15 = (bf16[1,512,512]{2,1,0:T(8,128)(2,1)S(1)}, bf16[1,512,512]{2,1,0:T(8,128)(2,1)S(1)}, u32[]{:S(2)}, u32[]{:S(2)}) collective-permute-start(bf16[1,512,512]{2,1,0:T(8,128)(2,1)S(1)} %attend_own.1), channel_id=1, source_target_pairs={{0,8},{8,0},{16,24},{24,16},{32,40},{40,32},{48,56},{56,48},{64,72... | collective-permute-start | bytes 1572872 | tf_op jit(solution)/shard_map/ppermute | solution.py:48
  57.9 22.0 %collective-permute-start.24 = (bf16[320,1024]{1,0:T(8,128)(2,1)S(1)}, bf16[320,1024]{1,0:T(8,128)(2,1)S(1)}, u32[]{:S(2)}, u32[]{:S(2)}) collective-permute-start(bf16[320,1024]{1,0:T(8,128)(2,1)S(1)} %collective-permute-done.1.refs_2_.refs_3_), channel_id=1, source_target_pairs={{0,16},{8,24},{16,32},{24,40},{32,48},{40,56},{48,0},{56,8},{64,80... | collective-permute-start | bytes 1966088 | tf_op jit(solution)/shard_map/ppermute | solution.py:48
  63.0 16.8 %collective-permute-start.25 = (bf16[320,1024]{1,0:T(8,128)(2,1)S(1)}, bf16[320,1024]{1,0:T(8,128)(2,1)S(1)}, u32[]{:S(2)}, u32[]{:S(2)}) collective-permute-start(bf16[320,1024]{1,0:T(8,128)(2,1)S(1)} %collective-permute-done.1.refs_2_.refs_3_), channel_id=1, source_target_pairs={{0,48},{8,56},{16,0},{24,8},{32,16},{40,24},{48,32},{56,40},{64,11... | collective-permute-start | bytes 1966088 | tf_op jit(solution)/shard_map/ppermute | solution.py:48
  65.1 15.7 %collective-permute-start.23 = (bf16[320,1024]{1,0:T(8,128)(2,1)S(1)}, bf16[320,1024]{1,0:T(8,128)(2,1)S(1)}, u32[]{:S(2)}, u32[]{:S(2)}) collective-permute-start(bf16[320,1024]{1,0:T(8,128)(2,1)S(1)} %constant_dynamic-update-slice_fusion.2.refs_0_.refs_1_), channel_id=1, source_target_pairs={{0,64},{8,72},{16,80},{24,88},{32,96},{40,104},{48,112},{56,120},{... | collective-permute-start | bytes 1966088 | tf_op jit(solution)/shard_map/ppermute | solution.py:48
  66.8 8.8 %collective-permute-start.20 = (bf16[640,256]{1,0:T(8,128)(2,1)S(1)}, bf16[640,256]{1,0:T(8,128)(2,1)S(1)}, u32[]{:S(2)}, u32[]{:S(2)}) collective-permute-start(bf16[640,256]{1,0:T(8,128)(2,1)S(1)} %far_low_early.1), channel_id=1, source_target_pairs={{0,6},{1,7},{2,0},{3,1},{4,2},{5,3},{6,4},{7,5},{8,14},{9,15},{10,... | collective-permute-start | bytes 983048 | tf_op jit(solution)/shard_map/ppermute | solution.py:52
  70.9 28.7 %collective-permute-start.16 = (bf16[640,256]{1,0:T(8,128)(2,1)S(1)}, bf16[640,256]{1,0:T(8,128)(2,1)S(1)}, u32[]{:S(2)}, u32[]{:S(2)}) collective-permute-start(bf16[640,256]{1,0:T(8,128)(2,1)S(1)} %far_top_early.1), channel_id=1, source_target_pairs={{0,2},{1,3},{2,4},{3,5},{4,6},{5,7},{6,0},{7,1},{8,10},{9,11},{10,... | collective-permute-start | bytes 983048 | tf_op jit(solution)/shard_map/ppermute | solution.py:52
  82.3 21.9 %collective-permute-start.26 = (bf16[640,256]{1,0:T(8,128)(2,1)S(1)}, bf16[640,256]{1,0:T(8,128)(2,1)S(1)}, u32[]{:S(2)}, u32[]{:S(2)}) collective-permute-start(bf16[640,256]{1,0:T(8,128)(2,1)S(1)} %far_top_late.1), channel_id=1, source_target_pairs={{0,2},{1,3},{2,4},{3,5},{4,6},{5,7},{6,0},{7,1},{8,10},{9,11},{10,... | collective-permute-start | bytes 983048 | tf_op jit(solution)/shard_map/ppermute | solution.py:52
  94.9 13.6 %collective-permute-start.30 = (bf16[640,256]{1,0:T(8,128)(2,1)S(1)}, bf16[640,256]{1,0:T(8,128)(2,1)S(1)}, u32[]{:S(2)}, u32[]{:S(2)}) collective-permute-start(bf16[640,256]{1,0:T(8,128)(2,1)S(1)} %far_low_late.1), channel_id=1, source_target_pairs={{0,6},{1,7},{2,0},{3,1},{4,2},{5,3},{6,4},{7,5},{8,14},{9,15},{10,... | collective-permute-start | bytes 983048 | tf_op jit(solution)/shard_map/ppermute | solution.py:52
  98.0 13.4 %collective-permute-start.18 = (bf16[640,256]{1,0:T(8,128)(2,1)S(1)}, bf16[640,256]{1,0:T(8,128)(2,1)S(1)}, u32[]{:S(2)}, u32[]{:S(2)}) collective-permute-start(bf16[640,256]{1,0:T(8,128)(2,1)S(1)} %down_top_early.1), channel_id=1, source_target_pairs={{0,6},{1,7},{2,0},{3,1},{4,2},{5,3},{6,4},{7,5},{8,14},{9,15},{10,... | collective-permute-start | bytes 983048 | tf_op jit(solution)/shard_map/ppermute | solution.py:52
  99.4 12.4 %collective-permute-start.19 = (bf16[640,256]{1,0:T(8,128)(2,1)S(1)}, bf16[640,256]{1,0:T(8,128)(2,1)S(1)}, u32[]{:S(2)}, u32[]{:S(2)}) collective-permute-start(bf16[640,256]{1,0:T(8,128)(2,1)S(1)} %up_low_early.1), channel_id=1, source_target_pairs={{0,2},{1,3},{2,4},{3,5},{4,6},{5,7},{6,0},{7,1},{8,10},{9,11},{10,... | collective-permute-start | bytes 983048 | tf_op jit(solution)/shard_map/ppermute | solution.py:52
  101.1 13.3 %collective-permute-start.17 = (bf16[640,256]{1,0:T(8,128)(2,1)S(1)}, bf16[640,256]{1,0:T(8,128)(2,1)S(1)}, u32[]{:S(2)}, u32[]{:S(2)}) collective-permute-start(bf16[640,256]{1,0:T(8,128)(2,1)S(1)} %up_top_early.1), channel_id=1, source_target_pairs={{0,2},{1,3},{2,4},{3,5},{4,6},{5,7},{6,0},{7,1},{8,10},{9,11},{10,... | collective-permute-start | bytes 983048 | tf_op jit(solution)/shard_map/ppermute | solution.py:52
  104.3 12.4 %collective-permute-start.21 = (bf16[640,256]{1,0:T(8,128)(2,1)S(1)}, bf16[640,256]{1,0:T(8,128)(2,1)S(1)}, u32[]{:S(2)}, u32[]{:S(2)}) collective-permute-start(bf16[640,256]{1,0:T(8,128)(2,1)S(1)} %down_low_early.1), channel_id=1, source_target_pairs={{0,6},{1,7},{2,0},{3,1},{4,2},{5,3},{6,4},{7,5},{8,14},{9,15},{10,... | collective-permute-start | bytes 983048 | tf_op jit(solution)/shard_map/ppermute | solution.py:52
  108.6 14.9 %collective-permute-start.28 = (bf16[640,256]{1,0:T(8,128)(2,1)S(1)}, bf16[640,256]{1,0:T(8,128)(2,1)S(1)}, u32[]{:S(2)}, u32[]{:S(2)}) collective-permute-start(bf16[640,256]{1,0:T(8,128)(2,1)S(1)} %down_top_late.1), channel_id=1, source_target_pairs={{0,6},{1,7},{2,0},{3,1},{4,2},{5,3},{6,4},{7,5},{8,14},{9,15},{10,... | collective-permute-start | bytes 983048 | tf_op jit(solution)/shard_map/ppermute | solution.py:52
  111.5 12.0 %collective-permute-start.29 = (bf16[640,256]{1,0:T(8,128)(2,1)S(1)}, bf16[640,256]{1,0:T(8,128)(2,1)S(1)}, u32[]{:S(2)}, u32[]{:S(2)}) collective-permute-start(bf16[640,256]{1,0:T(8,128)(2,1)S(1)} %up_low_late.1), channel_id=1, source_target_pairs={{0,2},{1,3},{2,4},{3,5},{4,6},{5,7},{6,0},{7,1},{8,10},{9,11},{10,... | collective-permute-start | bytes 983048 | tf_op jit(solution)/shard_map/ppermute | solution.py:52
  111.7 17.5 %collective-permute-start.27 = (bf16[640,256]{1,0:T(8,128)(2,1)S(1)}, bf16[640,256]{1,0:T(8,128)(2,1)S(1)}, u32[]{:S(2)}, u32[]{:S(2)}) collective-permute-start(bf16[640,256]{1,0:T(8,128)(2,1)S(1)} %up_top_late.1), channel_id=1, source_target_pairs={{0,2},{1,3},{2,4},{3,5},{4,6},{5,7},{6,0},{7,1},{8,10},{9,11},{10,... | collective-permute-start | bytes 983048 | tf_op jit(solution)/shard_map/ppermute | solution.py:52
  114.4 16.1 %collective-permute-start.31 = (bf16[640,256]{1,0:T(8,128)(2,1)S(1)}, bf16[640,256]{1,0:T(8,128)(2,1)S(1)}, u32[]{:S(2)}, u32[]{:S(2)}) collective-permute-start(bf16[640,256]{1,0:T(8,128)(2,1)S(1)} %down_low_late.1), channel_id=1, source_target_pairs={{0,6},{1,7},{2,0},{3,1},{4,2},{5,3},{6,4},{7,5},{8,14},{9,15},{10,... | collective-permute-start | bytes 983048 | tf_op jit(solution)/shard_map/ppermute | solution.py:52
  119.5 17.0 %collective-permute-start.22 = (bf16[1280,128]{1,0:T(8,128)(2,1)S(1)}, bf16[1280,128]{1,0:T(8,128)(2,1)S(1)}, u32[]{:S(2)}, u32[]{:S(2)}) collective-permute-start(bf16[1280,128]{1,0:T(8,128)(2,1)S(1)} %give_early.1), channel_id=1, source_target_pairs={{0,1},{1,0},{2,3},{3,2},{4,5},{5,4},{6,7},{7,6},{8,9},{9,8},{10,11... | collective-permute-start | bytes 983048 | tf_op jit(solution)/shard_map/ppermute | solution.py:52
  133.2 9.3 %collective-permute-start.32 = (bf16[1280,128]{1,0:T(8,128)(2,1)S(1)}, bf16[1280,128]{1,0:T(8,128)(2,1)S(1)}, u32[]{:S(2)}, u32[]{:S(2)}) collective-permute-start(bf16[1280,128]{1,0:T(8,128)(2,1)S(1)} %give_late.1), channel_id=1, source_target_pairs={{0,1},{1,0},{2,3},{3,2},{4,5},{5,4},{6,7},{7,6},{8,9},{9,8},{10,11... | collective-permute-start | bytes 983048 | tf_op jit(solution)/shard_map/ppermute | solution.py:52
  139.4 8.8 %collective-permute-start.33 = (bf16[1280,128]{1,0:T(8,128)(2,1)S(1)}, bf16[1280,128]{1,0:T(8,128)(2,1)S(1)}, u32[]{:S(2)}, u32[]{:S(2)}) collective-permute-start(bf16[1280,128]{1,0:T(8,128)(2,1)S(1)} %sum_early.1.refs_0_), channel_id=1, source_target_pairs={{0,8},{8,0},{16,24},{24,16},{32,40},{40,32},{48,56},{56,48},{64,72... | collective-permute-start | bytes 983048 | tf_op jit(solution)/shard_map/ppermute | solution.py:48
  (13 other events, 175.8 us)

commit v3 on v2

--- a/solution.py
+++ b/solution.py
@@ -41,6 +41,7 @@
 YFAR = sample_pairs(lambda z, y, c: (z, (y + 2) % 4, c))
 XUP = head_pairs(lambda x, z: ((x + 1) % 4, z))
 XDOWN = head_pairs(lambda x, z: ((x + 3) % 4, z))
+XFAR = head_pairs(lambda x, z: ((x + 2) % 4, z))
 ZHI = head_pairs(lambda x, z: (x, 1 - z))
 
 
@@ -209,33 +210,36 @@
 
 
 OTHER, OWN = False, True
+FEATURES = 320
 
 
 def project_kernel(tiles, count, spans, place_ref, *refs):
     weight_refs = refs[:2 * tiles]
     rows_refs = refs[2 * tiles:2 * tiles + 4 * count]
-    add_refs, out_ref = refs[2 * tiles + 4 * count:-1], refs[-1]
+    add_refs, out_ref, held_ref = refs[2 * tiles + 4 * count:-2], refs[-2], refs[-1]
     tile = pl.program_id(0)
     own = jnp.concatenate([r[...] for b in range(count) for r in rows_refs[4 * b:4 * b + 2]], axis=0)
     other = jnp.concatenate(
         [r[...] for b in range(count) for r in rows_refs[4 * b + 2:4 * b + 4]], axis=0
     )
 
-    def body(at):
-        acc = lax.dot_general(weight_refs[2 * at][...], own, NT, preferred_element_type=F32)
-        acc += lax.dot_general(weight_refs[2 * at + 1][...], other, NT, preferred_element_type=F32)
-        for ref, (start, length) in zip(add_refs, spans):
-            if start <= at < start + length:
-                acc += ref[...].astype(F32)
-        out_ref[...] = acc.astype(BF)
+    def bring(at):
+        held_ref[0] = weight_refs[2 * at][...]
+        held_ref[1] = weight_refs[2 * at + 1][...]
 
     for at in range(tiles):
-        pl.when(tile == at)(functools.partial(body, at))
-
-
-def project(place, weights, rows, blocks, adds, name):
+        pl.when(tile == at)(functools.partial(bring, at))
+    acc = lax.dot_general(held_ref[0], own, NT, preferred_element_type=F32)
+    acc += lax.dot_general(held_ref[1], other, NT, preferred_element_type=F32)
+    for ref, (start, length) in zip(add_refs, spans):
+        here = (tile >= start) & (tile < start + length)
+        acc += ref[...].astype(F32) if length == tiles else jnp.where(here, ref[...].astype(F32), 0.0)
+    out_ref[...] = acc.astype(out_ref.dtype)
+
+
+def project(place, weights, rows, blocks, adds, name, kind=BF):
     tiles = len(weights)
-    size = weights[0].shape[0]
+    size = FEATURES
     part, depth = rows[0].shape[1:]
     lanes = 2 * part * len(blocks)
 
@@ -252,9 +256,9 @@
         )
 
     in_specs, args = [], []
-    for weight in weights:
-        in_specs.append(pl.BlockSpec((size, depth), lambda i, p: (0, p[CORE_AT])))
-        in_specs.append(pl.BlockSpec((size, depth), lambda i, p: (0, 1 - p[CORE_AT])))
+    for weight, at in weights:
+        in_specs.append(pl.BlockSpec((size, depth), lambda i, p, at=at: (at, p[CORE_AT])))
+        in_specs.append(pl.BlockSpec((size, depth), lambda i, p, at=at: (at, 1 - p[CORE_AT])))
         args += [weight, weight]
     for block in blocks:
         in_specs += [rows_spec(*block)] * 4
@@ -269,8 +273,9 @@
             grid=(tiles,),
             in_specs=in_specs,
             out_specs=pl.BlockSpec((size, lanes), lambda i, p: (i, 0)),
-        ),
-        out_shape=jax.ShapeDtypeStruct((tiles * size, lanes), BF),
+            scratch_shapes=[pltpu.VMEM((2, size, depth), BF)],
+        ),
+        out_shape=jax.ShapeDtypeStruct((tiles * size, lanes), kind),
         name=name,
         cost_estimate=pl.CostEstimate(
             flops=4 * tiles * size * lanes * depth,
@@ -281,68 +286,118 @@
     )(place, *args)
 
 
-def sum_over_head(place, weights, rows, tag):
-    run = lambda w, blocks, adds, name: project(place, w, rows, blocks, adds, name + tag)
+def gather_kernel(count, base_ref, *refs):
+    out_ref = refs[-1]
+    halves, whole = refs[:-1 - count], refs[-1 - count:-1]
+    lines = base_ref.shape[0] // 2
+    for half in range(2):
+        at = slice(half * lines, (half + 1) * lines)
+        acc = base_ref[at]
+        for ref in halves[half::2]:
+            acc += ref[...].astype(F32)
+        for ref in whole:
+            acc += ref[at].astype(F32)
+        out_ref[at] = acc.astype(BF)
+
+
+def gather(base, lane, halves, whole, name):
+    lines = base.shape[0]
+    halves = [array for pair in halves for array in pair]
+    spec = lambda size, at: pl.BlockSpec((size, 128), lambda i: (0, at))
+    return pl.pallas_call(
+        functools.partial(gather_kernel, len(whole)),
+        grid=(1,),
+        in_specs=[spec(lines, lane)] + [spec(lines // 2, lane)] * len(halves)
+        + [spec(lines, 0)] * len(whole),
+        out_specs=spec(lines, 0),
+        out_shape=jax.ShapeDtypeStruct((lines, 128), BF),
+        name=name,
+        cost_estimate=pl.CostEstimate(
+            flops=6 * lines * 128, bytes_accessed=20 * lines * 128, transcendentals=0
+        ),
+        compiler_params=pltpu.CompilerParams(vmem_limit_bytes=32 * 2**20),
+    )(base, *halves, *whole)
+
+
+def sum_over_head(place, weights, rows, tag, beside=()):
+    run = lambda w, blocks, adds, name, kind=BF: project(
+        place, w, rows, blocks, adds, name + tag, kind
+    )
     both = lambda step: [(step, OTHER), (step, OWN)]
     n = len(weights) // 2
     top, low = weights[:n], weights[n:]
     via_up = over_head(run(top, both(2), [], "far_top"), XUP)
     via_down = over_head(run(low, both(2), [], "far_low"), XDOWN)
+    via_up, via_down, beside = lax.optimization_barrier((via_up, via_down, beside))
     below_low = over_head(run(low, both(1), [], "up_low"), XUP)
     above_top = over_head(run(top, both(3), [], "down_top"), XDOWN)
     below_top = over_head(run(top, both(1), [(via_up, 0, 0, n)], "up_top"), XUP)
-    last = run(low, both(3), [(via_down, 0, 0, n)], "down_low")
-    above_low = over_head(last, XDOWN)
-
-    def arrived(lane):
-        return [
-            (below_top, lane, 0, n), (above_top, lane, 0, n),
-            (below_low, lane, n, n), (above_low, lane, n, n),
-        ]
-
-    from_z = over_head(run(weights, [(0, OTHER)], arrived(0), "give"), ZHI)
-    return run(weights, [(0, OWN)], arrived(1) + [(from_z, 0, 0, 2 * n)], "sum"), last
-
-
-SPOTS = ((0, 3, 4, 2), (1, 7, 5, 6))
-
-
-def finish_kernel(cols, blocks, place_ref, spot_ref, *refs):
-    own_refs, got_refs, out_ref = refs[:2], refs[2:4], refs[4]
+    above_low = over_head(run(low, both(3), [(via_down, 0, 0, n)], "down_low"), XDOWN)
+    own = run(weights, both(0), [], "own", F32)
+    arrived = [(below_top, below_low), (above_top, above_low)]
+    from_z = over_head(gather(own, 0, arrived, [], "give" + tag), ZHI)
+    return from_z, lambda from_z: gather(own, 1, arrived, [from_z], "sum" + tag), beside
+
+
+def give_z_first(place, weights, rows, tag):
+    return project(place, weights, rows, [(step, OTHER) for step in range(4)], [], "give" + tag)
+
+
+def sum_z_first(place, weights, rows, got, tag):
+    part = lambda step, name, kind: project(
+        place, weights, rows, [(step, OWN)], [(got, step, 0, len(weights))], name + tag, kind
+    )
+    sends = [(part(step, name, BF), to) for step, name, to in FAR_UP_DOWN]
+    return sends, part(0, "own", F32)
+
+
+FAR_UP_DOWN = ((2, "far", XFAR), (1, "up", XUP), (3, "down", XDOWN))
+
+
+EARLY_FROM = ((0, 0), (1, 0), (0, 3), (1, 3), (0, 1), (1, 1))
+LATE_FROM = ((0, 2), (1, 2))
+
+
+def finish_kernel(place_ref, from_ref, own_ref, got_ref, *refs):
+    out_ref = refs[-1]
     lane = lax.broadcasted_iota(jnp.int32, (64, 128), 1)
     row = lax.broadcasted_iota(jnp.int32, (64, 128), 0)
     turn = lambda array, at: lax.dot_general(
         jnp.where(lane == row + at, 1.0, 0.0).astype(BF), array, NT, preferred_element_type=F32
     )
+    own, got = turn(own_ref[...], 0), turn(got_ref[...], 64)
     first = place_ref[CORE_AT] == 0
-    count = len(SPOTS) * len(SPOTS[0]) // 2
-    for b in range(blocks):
-        i = pl.program_id(0) * blocks + b
-        dz = lax.rem(i // 4 + place_ref[Z_LO], 2)
-        dy = lax.rem(lax.rem(i, 4) + 4 - place_ref[Y], 4)
-        spot = spot_ref[dz * 4 + dy]
-        lines = pl.ds(pl.multiple_of(lax.rem(spot, count) * cols, cols), cols)
-        take = lambda pair: jnp.where(spot < count, pair[0][lines], pair[1][lines])
-        own, got = turn(take(own_refs), 0), turn(take(got_refs), 64)
-        even, odd = jnp.where(first, own, got), jnp.where(first, got, own)
-        out_ref[:, b * 2 * cols:(b + 1) * 2 * cols] = jnp.concatenate([even, odd], axis=1).astype(BF)
-
-
-def finish(place, own, got, cols):
-    spots = jnp.array([s for line in SPOTS for s in line], jnp.int32)
-    whole = pl.BlockSpec(own[0].shape, lambda i, p, s: (0, 0))
-    blocks = 4
+    even, odd = jnp.where(first, own, got), jnp.where(first, got, own)
+    out_ref[...] = jnp.concatenate([even, odd], axis=1).astype(BF)
+
+
+def finish(place, own, got, chips, out, name):
+    wide = 2 * FEATURES
+    offsets = jnp.array([d for chip in chips for d in chip], jnp.int32)
+
+    def to(i, p, f):
+        z = lax.rem(f[2 * i] + p[Z_LO], 2)
+        return (0, z * 4 + lax.rem(f[2 * i + 1] + p[Y], 4))
+
+    part = pl.BlockSpec((FEATURES, 128), lambda i, p, f: (i, 0))
     return pl.pallas_call(
-        functools.partial(finish_kernel, cols, blocks),
+        finish_kernel,
         grid_spec=pltpu.PrefetchScalarGridSpec(
             num_scalar_prefetch=2,
-            grid=(8 // blocks,),
-            in_specs=[whole] * 4,
-            out_specs=pl.BlockSpec((64, blocks * 2 * cols), lambda i, p, s: (0, i)),
-        ),
-        out_shape=jax.ShapeDtypeStruct((64, 16 * cols), BF),
-        name="finish",
-    )(place, spots, *own, *got)
+            grid=(len(chips),),
+            in_specs=[part, part] + [pl.BlockSpec(memory_space=pl.ANY)] * len(out),
+            out_specs=pl.BlockSpec((64, wide), to),
+        ),
+        out_shape=jax.ShapeDtypeStruct((64, 8 * wide), BF),
+        input_output_aliases={4: 0} if out else {},
+        name=name,
+        cost_estimate=pl.CostEstimate(
+            flops=len(chips) * 2 * 64 * 128 * wide,
+            bytes_accessed=len(chips) * wide * 400,
+            transcendentals=0,
+        ),
+        compiler_params=pltpu.CompilerParams(vmem_limit_bytes=32 * 2**20),
+    )(place, offsets, own, got, *out)
 
 
 def per_device(
@@ -365,42 +420,45 @@
     suffix = [suffix_keys[0], suffix_values[0]]
     suffixes = suffix + [over_sample(a, CORE) for a in suffix]
     kv_core = over_sample(kv, CORE)
+    w, kv_z = hold((out_weight.T, kv_z))
+    w_z = over_sample(w, ZLO)
     near = jnp.stack([kv, kv_z])
     ys = [over_sample(near, to) for to in (YUP, YDOWN, YFAR)]
 
-    w, near = hold((out_weight.T, near))
-    w_z = over_sample(w, ZLO)
-
     run = lambda kvs, state, samples, last, name: attend(
         place, q_own, q_got, suffixes, kvs, state, samples, last, name
     )
     state = run([kv[None], kv_core[None]], None, (0, 1), False, "attend_near")
-    ys, state, w_y, wz_y = hold((ys, state, w, w_z))
-    w_up, w_down = over_sample(w_y, YUP), over_sample(w_y, YDOWN)
-    wz_up, wz_down = over_sample(wz_y, YUP), over_sample(wz_y, YDOWN)
+    ys, state, w_z = hold((ys, state, w_z))
+    w_pair = jnp.concatenate([w, w_z], axis=0)
+    w_up, w_down = over_sample(w_pair, YUP), over_sample(w_pair, YDOWN)
     rest = [jnp.concatenate([kv_z[None]] + ys, axis=0)]
     rest_core = [over_sample(rest[0], CORE)]
     state = run(rest, state, (0, 1), False, "attend_far")
-    state, w_up, w_down = hold((state, w_up, w_down))
-    half_lines = w.shape[0] // 2
-    far_up = over_sample(w_up[:half_lines], YUP)
-    far_down = over_sample(w_down[half_lines:], YDOWN)
     own = run(rest_core, state, (0,), True, "attend_own")
     own_core = over_sample(own, CORE)
     state, own = hold((state, own))
     partner = run(rest_core, state, (1,), True, "attend_partner")
     partner_core = over_sample(partner, CORE)
-    partner, far_up, far_down = hold((partner, far_up, far_down))
-    w_far = jnp.concatenate([far_up, far_down], axis=0)
-    wz_far = over_sample(w_far, ZLO)
+    partner, w_up, w_down = hold((partner, w_up, w_down))
+    w_far = over_sample(w_up[:FEATURES], YUP)
+    wz_far = over_sample(w_down[FEATURES:], YDOWN)
 
     rows = [a.reshape(8, 64, width) for a in (own, partner, partner_core, own_core)]
-    early, after = sum_over_head(place, [w, w_z, w_up, w_down], rows, "_early")
-    w_late, _ = hold(([w_far, wz_far, wz_up, wz_down], after))
-    late, _ = sum_over_head(place, w_late, rows, "_late")
-
-    got = [over_sample(early, CORE), over_sample(late, CORE)]
-    return finish(place, [early, late], got, out_weight.shape[1])[None]
+    w_early = [(w_pair, 0), (w_pair, 1), (w_up, 0), (w_up, 1), (w_down, 0), (w_down, 1)]
+    w_late = [(w_far, 0), (wz_far, 0)]
+    give_late = give_z_first(place, w_late, rows, "_late")
+    from_z, finish_early, give_late = sum_over_head(place, w_early, rows, "_early", give_late)
+    got = over_head(give_late, ZHI)
+    sends, own = sum_z_first(place, w_late, rows, got, "_late")
+    arrived = [over_head(part, to) for part, to in sends]
+    from_z, arrived = hold((from_z, arrived))
+    early = finish_early(from_z)
+    late = gather(own, 0, [], arrived, "sum_late")
+
+    out = finish(place, early, over_sample(early, CORE), EARLY_FROM, [], "finish_early")
+    out = finish(place, late, over_sample(late, CORE), LATE_FROM, [out], "finish_late")
+    return out[None]
 
 
 def solution(mesh):

time: 156 us -> 133 us (0.85); the launches traced: 154 us -> 134 us
  starting transfers between devices: 66.1 us -> 44.6 us
  Pallas kernels: 53.1 us -> 58.7 us
  waiting for transfers between devices: 24.4 us -> 21 us
  local copies, waits for them, and re-layouts: 9.63 us -> 7 us
  other arithmetic: 0.14 us -> 1.94 us
    ppermute x14 -> x11, starting transfers between devices: 30.2 us -> 19.3 us  [over_head(): return lax.ppermute(value, 'head', pairs)]
    ppermute x21 -> x18, starting transfers between devices: 35.9 us -> 25.4 us  [over_sample(): return lax.ppermute(value, 'sample', pairs)]
    pallas_call x4, Pallas kernels: 19.9 us -> 26.4 us  [attend(): pl.pallas_call(functools.partial(attend_kernel, counts, samples, first, l...]
    ppermute x14 -> x11, waiting for transfers between devices: 13.3 us -> 9.21 us  [over_head(): return lax.ppermute(value, 'head', pairs)]
    pallas_call x16 -> x12, Pallas kernels: 29.6 us -> 25.9 us  [project(): pl.pallas_call(functools.partial(project_kernel, tiles, len(blocks), [a[2...]
    pallas_call x1 -> x5, Pallas kernels: 3.58 us -> 6.34 us  [the longest x2 5.31 us: finish(): pl.pallas_call(finish_kernel, grid_spec=pltpu.PrefetchScalarGridSpec(num_...]
    unnamed x22 -> x16, local copies, waits for them, and re-layouts: 6 us -> 3.37 us
    ppermute x21 -> x18, waiting for transfers between devices: 11.2 us -> 11.8 us  [over_sample(): return lax.ppermute(value, 'sample', pairs)]
  transfers between devices with their start and end apart: 35 -> 29, of which waited for: 12 -> 8; matrix products, arithmetic and copies ran while one was open for 3% -> 6% of each run, Pallas kernels for 32% -> 42%
where the time goes in v3:
time: 133 us; the launch traced here: 134 us
  Pallas kernels  58.7 us (44%)
  starting transfers between devices  44.6 us (34%)
  waiting for transfers between devices  21 us (16%)
  local copies, waits for them, and re-layouts  7 us (5%)
  other arithmetic  1.94 us (1%)
    pallas_call x4, Pallas kernels, attend(): pl.pallas_call(functools.partial(attend_kernel, counts, samples, first, l...  26.4 us
    pallas_call x12, Pallas kernels, project(): pl.pallas_call(functools.partial(project_kernel, tiles, len(blocks), [a[2...  25.9 us
    ppermute x18, starting transfers between devices, over_sample(): return lax.ppermute(value, 'sample', pairs)  25.4 us
    ppermute x11, starting transfers between devices, over_head(): return lax.ppermute(value, 'head', pairs)  19.3 us
    ppermute x18, waiting for transfers between devices, over_sample(): return lax.ppermute(value, 'sample', pairs)  11.8 us
    ppermute x11, waiting for transfers between devices, over_head(): return lax.ppermute(value, 'head', pairs)  9.21 us
    pallas_call x2, Pallas kernels, finish(): pl.pallas_call(finish_kernel, grid_spec=pltpu.PrefetchScalarGridSpec(num_...  5.31 us
    unnamed x16, local copies, waits for them, and re-layouts  3.37 us
  transfers between devices with their start and end apart: 29, of which 8 were waited for; matrix products, arithmetic and copies ran while one was open for 6% of the time, Pallas kernels for 42%

profile of v3, /device:TPU:1, one launch (start us, length us, event | category | flops | bytes accessed | tf_op | source)
XLA Modules:
  0.0 133.5 jit_solution(2025476794168031003)
XLA Ops:
  3.2 1.8 %collective-permute-start.1 = (bf16[256,256]{1,0:T(8,128)(2,1)S(1)}, bf16[256,256]{1,0:T(8,128)(2,1)}, u32[]{:S(2)}, u32[]{:S(2)}) collective-permute-start(bf16[256,256]{1,0:T(8,128)(2,1)S(1)} %constant_dynamic-update-slice_fusion), channel_id=1, source_target_pairs={{0,64},{8,72},{16,80},{24,88},{32,96},{40,104},{48,112},{56,120},{... | collective-permute-start | bytes 393224 | tf_op jit(solution)/shard_map/ppermute | solution.py:49
  9.9 2.9 %collective-permute-start.4 = (bf16[2,256,256]{2,1,0:T(8,128)(2,1)S(1)}, bf16[2,256,256]{2,1,0:T(8,128)(2,1)S(1)}, u32[]{:S(2)}, u32[]{:S(2)}) collective-permute-start(bf16[2,256,256]{2,1,0:T(8,128)(2,1)S(1)} %pad_maximum_fusion.1), channel_id=1, source_target_pairs={{0,32},{8,40},{16,48},{24,56},{32,0},{40,8},{48,16},{56,24},{64,96... | collective-permute-start | bytes 786440 | tf_op jit(solution)/shard_map/ppermute | solution.py:49
  16.7 5.2 %attend_near.1 = (f32[2,512,512]{2,1,0:T(8,128)S(1)}, f32[2,512,128]{2,1,0:T(8,128)S(1)}) custom-call(s32[7]{0:T(128)S(1)} %stack.30.place_ref, bf16[512,1024]{1,0:T(8,128)(2,1)S(1)} %bitcast.108, bf16[512,1024]{1,0:T(8,128)(2,1)S(1)} %collective-permute-done.q_got_ref, bf16[512,128]{1,0:T(8,128)(2,1)S(1)} %bitcast.113, bf16[512,128]{1,0:T(8,128)(2,1)S(1)} %bitcast.115, ...), custom_call_target="tpu_custom_call" | custom-call | flops 12884901888 | bytes 8388608 | tf_op jit(solution)/shard_map/attend_near/pallas_call | solution.py:189
  24.5 5.5 %collective-permute-done.8 = bf16[320,1024]{1,0:T(8,128)(2,1)S(1)} collective-permute-done((bf16[320,1024]{1,0:T(8,128)(2,1)S(1)}, bf16[320,1024]{1,0:T(8,128)(2,1)S(1)}, u32[]{:S(2)}, u32[]{:S(2)}) %collective-permute-start.8) | collective-permute-done | bytes 655392 | tf_op jit(solution)/shard_map/ppermute | solution.py:49
  30.1 2.1 %collective-permute-start.11 = (bf16[640,1024]{1,0:T(8,128)(2,1)S(1)}, bf16[640,1024]{1,0:T(8,128)(2,1)S(1)}, u32[]{:S(2)}, u32[]{:S(2)}) collective-permute-start(bf16[640,1024]{1,0:T(8,128)(2,1)S(1)} %constant_dynamic-update-slice_fusion.2.refs_0_.refs_1_.refs_2_.refs_3_), channel_id=1, source_target_pairs={{0,48},{8,56},{16,0},{24,8},{32,16},{40,24},{48,32},{56,40},{64,11... | collective-permute-start | bytes 3932168 | tf_op jit(solution)/shard_map/ppermute | solution.py:49
  33.2 3.1 %collective-permute-start.9 = (bf16[7,256,256]{2,1,0:T(8,128)(2,1)S(1)}, bf16[7,256,256]{2,1,0:T(8,128)(2,1)S(1)}, u32[]{:S(2)}, u32[]{:S(2)}) collective-permute-start(bf16[7,256,256]{2,1,0:T(8,128)(2,1)S(1)} %pad_maximum_fusion.refs_0_), channel_id=1, source_target_pairs={{0,8},{8,0},{16,24},{24,16},{32,40},{40,32},{48,56},{56,48},{64,72... | collective-permute-start | bytes 2752520 | tf_op jit(solution)/shard_map/ppermute | solution.py:49
  36.2 10.8 %attend_far.1 = (f32[2,512,512]{2,1,0:T(8,128)S(1)}, f32[2,512,128]{2,1,0:T(8,128)S(1)}) custom-call(s32[7]{0:T(128)S(1)} %stack.30.place_ref, bf16[512,1024]{1,0:T(8,128)(2,1)S(1)} %bitcast.109, bf16[512,1024]{1,0:T(8,128)(2,1)S(1)} %collective-permute-done.q_got_ref, bf16[7,256,256]{2,1,0:T(8,128)(2,1)S(1)} %pad_maximum_fusion.refs_0_, ...), custom_call_target="tpu_custom_call" | custom-call | flops 30064771072 | bytes 8388608 | tf_op jit(solution)/shard_map/attend_far/pallas_call | solution.py:189
  47.1 6.6 %attend_own.1 = bf16[1,512,512]{2,1,0:T(8,128)(2,1)S(1)} custom-call(s32[7]{0:T(128)S(1)} %stack.30.place_ref, bf16[512,1024]{1,0:T(8,128)(2,1)S(1)} %bitcast.110, bf16[512,1024]{1,0:T(8,128)(2,1)S(1)} %collective-permute-done.q_got_ref, bf16[7,256,256]{2,1,0:T(8,128)(2,1)S(1)} %collective-permute-done.9.refs_0_, ...), custom_call_target="tpu_custom_call" | custom-call | flops 15032385536 | bytes 4194304 | tf_op jit(solution)/shard_map/attend_own/pallas_call | solution.py:189
  53.7 3.8 %attend_partner.1 = bf16[1,512,512]{2,1,0:T(8,128)(2,1)S(1)} custom-call(s32[7]{0:T(128)S(1)} %stack.30.place_ref, bf16[512,1024]{1,0:T(8,128)(2,1)S(1)} %bitcast.111, bf16[512,1024]{1,0:T(8,128)(2,1)S(1)} %collective-permute-done.q_got_ref, bf16[7,256,256]{2,1,0:T(8,128)(2,1)S(1)} %collective-permute-done.9.refs_0_, ...), custom_call_target="tpu_custom_call" | custom-call | flops 15032385536 | bytes 4194304 | tf_op jit(solution)/shard_map/attend_partner/pallas_call | solution.py:189
  58.6 2.2 %collective-permute-done.10.refs_4_.refs_5_.refs_0_.refs_1_.refs_6_.refs_7_ = bf16[640,1024]{1,0:T(8,128)(2,1)S(1)} collective-permute-done((bf16[640,1024]{1,0:T(8,128)(2,1)S(1)}, bf16[640,1024]{1,0:T(8,128)(2,1)S(1)}, u32[]{:S(2)}, u32[]{:S(2)}) %collective-permute-start.10) | collective-permute-done | bytes 1310752 | tf_op jit(solution)/shard_map/ppermute | solution.py:49
  61.0 6.1 %collective-permute-start.13 = (bf16[320,1024]{1,0:T(8,128)(2,1)S(1)}, bf16[320,1024]{1,0:T(8,128)(2,1)S(1)}, u32[]{:S(2)}, u32[]{:S(2)}) collective-permute-start(bf16[320,1024]{1,0:T(8,128)(2,1)S(1)} %slice.7), channel_id=1, source_target_pairs={{0,48},{8,56},{16,0},{24,8},{32,16},{40,24},{48,32},{56,40},{64,11... | collective-permute-start | bytes 1966088 | tf_op jit(solution)/shard_map/ppermute | solution.py:49
  67.1 2.2 %far_low_early.1 = bf16[960,256]{1,0:T(8,128)(2,1)S(1)} custom-call(s32[7]{0:T(128)S(1)} %stack.30.place_ref, bf16[640,1024]{1,0:T(8,128)(2,1)S(1)} %collective-permute-done.10.refs_4_.refs_5_.refs_0_.refs_1_.refs_6_.refs_7_, bf16[640,1024]{1,0:T(8,128)(2,1)S(1)} %collective-permute-done.10.refs_4_.refs_5_.refs_0_.refs_1_.refs_6_.refs_7_, ...), custom_call_target="tpu_custom_call" | custom-call | flops 503316480 | bytes 2457600 | tf_op jit(solution)/shard_map/far_low_early/pallas_call | solution.py:269
  69.3 2.2 %far_top_early.1 = bf16[960,256]{1,0:T(8,128)(2,1)S(1)} custom-call(s32[7]{0:T(128)S(1)} %stack.30.place_ref, bf16[640,1024]{1,0:T(8,128)(2,1)S(1)} %constant_dynamic-update-slice_fusion.2.refs_0_.refs_1_.refs_2_.refs_3_, bf16[640,1024]{1,0:T(8,128)(2,1)S(1)} %constant_dynamic-update-slice_fusion.2.refs_0_.refs_1_.refs_2_.refs_3_, ...), custom_call_target="tpu_custom_call" | custom-call | flops 503316480 | bytes 2457600 | tf_op jit(solution)/shard_map/far_top_early/pallas_call | solution.py:269
  74.4 2.2 %up_low_early.1 = bf16[960,256]{1,0:T(8,128)(2,1)S(1)} custom-call(s32[7]{0:T(128)S(1)} %stack.30.place_ref, bf16[640,1024]{1,0:T(8,128)(2,1)S(1)} %collective-permute-done.10.refs_4_.refs_5_.refs_0_.refs_1_.refs_6_.refs_7_, bf16[640,1024]{1,0:T(8,128)(2,1)S(1)} %collective-permute-done.10.refs_4_.refs_5_.refs_0_.refs_1_.refs_6_.refs_7_, ...), custom_call_target="tpu_custom_call" | custom-call | flops 503316480 | bytes 2457600 | tf_op jit(solution)/shard_map/up_low_early/pallas_call | solution.py:269
  76.7 2.2 %down_top_early.1 = bf16[960,256]{1,0:T(8,128)(2,1)S(1)} custom-call(s32[7]{0:T(128)S(1)} %stack.30.place_ref, bf16[640,1024]{1,0:T(8,128)(2,1)S(1)} %constant_dynamic-update-slice_fusion.2.refs_0_.refs_1_.refs_2_.refs_3_, bf16[640,1024]{1,0:T(8,128)(2,1)S(1)} %constant_dynamic-update-slice_fusion.2.refs_0_.refs_1_.refs_2_.refs_3_, ...), custom_call_target="tpu_custom_call" | custom-call | flops 503316480 | bytes 2457600 | tf_op jit(solution)/shard_map/down_top_early/pallas_call | solution.py:269
  78.9 2.5 %collective-permute-done.12.refs_0_.refs_1_ = bf16[320,1024]{1,0:T(8,128)(2,1)S(1)} collective-permute-done((bf16[320,1024]{1,0:T(8,128)(2,1)S(1)}, bf16[320,1024]{1,0:T(8,128)(2,1)S(1)}, u32[]{:S(2)}, u32[]{:S(2)}) %collective-permute-start.12) | collective-permute-done | bytes 655392 | tf_op jit(solution)/shard_map/ppermute | solution.py:49
  81.4 2.5 %collective-permute-start.21 = (bf16[960,256]{1,0:T(8,128)(2,1)S(1)}, bf16[960,256]{1,0:T(8,128)(2,1)S(1)}, u32[]{:S(2)}, u32[]{:S(2)}) collective-permute-start(bf16[960,256]{1,0:T(8,128)(2,1)S(1)} %down_top_early.1), channel_id=1, source_target_pairs={{0,6},{1,7},{2,0},{3,1},{4,2},{5,3},{6,4},{7,5},{8,14},{9,15},{10,... | collective-permute-start | bytes 1474568 | tf_op jit(solution)/shard_map/ppermute | solution.py:53
  83.9 2.1 %give_late.1 = bf16[640,512]{1,0:T(8,128)(2,1)S(1)} custom-call(s32[7]{0:T(128)S(1)} %stack.30.place_ref, bf16[320,1024]{1,0:T(8,128)(2,1)S(1)} %collective-permute-done.12.refs_0_.refs_1_, bf16[320,1024]{1,0:T(8,128)(2,1)S(1)} %collective-permute-done.12.refs_0_.refs_1_, bf16[320,1024]{1,0:T(8,128)(2,1)S(1)} %collective-permute-done.13.refs_2_.refs_3_, ...), custom_call_target="tpu_custom_call" | custom-call | flops 671088640 | bytes 1966080 | tf_op jit(solution)/shard_map/give_late/pallas_call | solution.py:269
  86.0 2.2 %up_top_early.1 = bf16[960,256]{1,0:T(8,128)(2,1)S(1)} custom-call(s32[7]{0:T(128)S(1)} %stack.30.place_ref, bf16[640,1024]{1,0:T(8,128)(2,1)S(1)} %constant_dynamic-update-slice_fusion.2.refs_0_.refs_1_.refs_2_.refs_3_, bf16[640,1024]{1,0:T(8,128)(2,1)S(1)} %constant_dynamic-update-slice_fusion.2.refs_0_.refs_1_.refs_2_.refs_3_, ...), custom_call_target="tpu_custom_call" | custom-call | flops 503316480 | bytes 2457600 | tf_op jit(solution)/shard_map/up_top_early/pallas_call | solution.py:269
  88.2 2.2 %down_low_early.1 = bf16[960,256]{1,0:T(8,128)(2,1)S(1)} custom-call(s32[7]{0:T(128)S(1)} %stack.30.place_ref, bf16[640,1024]{1,0:T(8,128)(2,1)S(1)} %collective-permute-done.10.refs_4_.refs_5_.refs_0_.refs_1_.refs_6_.refs_7_, bf16[640,1024]{1,0:T(8,128)(2,1)S(1)} %collective-permute-done.10.refs_4_.refs_5_.refs_0_.refs_1_.refs_6_.refs_7_, ...), custom_call_target="tpu_custom_call" | custom-call | flops 503316480 | bytes 2457600 | tf_op jit(solution)/shard_map/down_low_early/pallas_call | solution.py:269
  92.0 3.5 %collective-permute-start.18 = (bf16[640,512]{1,0:T(8,128)(2,1)S(1)}, bf16[640,512]{1,0:T(8,128)(2,1)S(1)}, u32[]{:S(2)}, u32[]{:S(2)}) collective-permute-start(bf16[640,512]{1,0:T(8,128)(2,1)S(1)} %give_late.1), channel_id=1, source_target_pairs={{0,1},{1,0},{2,3},{3,2},{4,5},{5,4},{6,7},{7,6},{8,9},{9,8},{10,11... | collective-permute-start | bytes 1966088 | tf_op jit(solution)/shard_map/ppermute | solution.py:53
  95.5 4.2 %own_early.1.base_ref = f32[1920,256]{1,0:T(8,128)S(1)} custom-call(s32[7]{0:T(128)S(1)} %stack.30.place_ref, bf16[640,1024]{1,0:T(8,128)(2,1)S(1)} %constant_dynamic-update-slice_fusion.2.refs_0_.refs_1_.refs_2_.refs_3_, bf16[640,1024]{1,0:T(8,128)(2,1)S(1)} %constant_dynamic-update-slice_fusion.2.refs_0_.refs_1_.refs_2_.refs_3_, ...), custom_call_target="tpu_custom_call" | custom-call | flops 1006632960 | bytes 4915200 | tf_op jit(solution)/shard_map/own_early/pallas_call | solution.py:269
  99.7 5.9 %collective-permute-done.22.refs_3_ = bf16[960,256]{1,0:T(8,128)(2,1)S(1)} collective-permute-done((bf16[960,256]{1,0:T(8,128)(2,1)S(1)}, bf16[960,256]{1,0:T(8,128)(2,1)S(1)}, u32[]{:S(2)}, u32[]{:S(2)}) %collective-permute-start.22) | collective-permute-done | bytes 491552 | tf_op jit(solution)/shard_map/ppermute | solution.py:53
  106.0 3.5 %collective-permute-start.23 = (bf16[1920,128]{1,0:T(8,128)(2,1)S(1)}, bf16[1920,128]{1,0:T(8,128)(2,1)S(1)}, u32[]{:S(2)}, u32[]{:S(2)}) collective-permute-start(bf16[1920,128]{1,0:T(8,128)(2,1)S(1)} %give_early.1), channel_id=1, source_target_pairs={{0,1},{1,0},{2,3},{3,2},{4,5},{5,4},{6,7},{7,6},{8,9},{9,8},{10,11... | collective-permute-start | bytes 1474568 | tf_op jit(solution)/shard_map/ppermute | solution.py:53
  111.1 2.5 %collective-permute-start.24 = (bf16[640,128]{1,0:T(8,128)(2,1)S(1)}, bf16[640,128]{1,0:T(8,128)(2,1)S(1)}, u32[]{:S(2)}, u32[]{:S(2)}) collective-permute-start(bf16[640,128]{1,0:T(8,128)(2,1)S(1)} %far_late.1), channel_id=1, source_target_pairs={{0,4},{1,5},{2,6},{3,7},{4,0},{5,1},{6,2},{7,3},{8,12},{9,13},{10,... | collective-permute-start | bytes 491528 | tf_op jit(solution)/shard_map/ppermute | solution.py:53
  113.6 1.6 %up_late.1 = bf16[640,128]{1,0:T(8,128)(2,1)S(1)} custom-call(s32[7]{0:T(128)S(1)} %stack.30.place_ref, bf16[320,1024]{1,0:T(8,128)(2,1)S(1)} %collective-permute-done.12.refs_0_.refs_1_, bf16[320,1024]{1,0:T(8,128)(2,1)S(1)} %collective-permute-done.12.refs_0_.refs_1_, bf16[320,1024]{1,0:T(8,128)(2,1)S(1)} %collective-permute-done.13.refs_2_.refs_3_, ...), custom_call_target="tpu_custom_call" | custom-call | flops 167772160 | bytes 1474560 | tf_op jit(solution)/shard_map/up_late/pallas_call | solution.py:269
  115.2 1.6 %collective-permute-start.25 = (bf16[640,128]{1,0:T(8,128)(2,1)S(1)}, bf16[640,128]{1,0:T(8,128)(2,1)S(1)}, u32[]{:S(2)}, u32[]{:S(2)}) collective-permute-start(bf16[640,128]{1,0:T(8,128)(2,1)S(1)} %up_late.1), channel_id=1, source_target_pairs={{0,2},{1,3},{2,4},{3,5},{4,6},{5,7},{6,0},{7,1},{8,10},{9,11},{10,... | collective-permute-start | bytes 491528 | tf_op jit(solution)/shard_map/ppermute | solution.py:53
  116.8 1.6 %down_late.1 = bf16[640,128]{1,0:T(8,128)(2,1)S(1)} custom-call(s32[7]{0:T(128)S(1)} %stack.30.place_ref, bf16[320,1024]{1,0:T(8,128)(2,1)S(1)} %collective-permute-done.12.refs_0_.refs_1_, bf16[320,1024]{1,0:T(8,128)(2,1)S(1)} %collective-permute-done.12.refs_0_.refs_1_, bf16[320,1024]{1,0:T(8,128)(2,1)S(1)} %collective-permute-done.13.refs_2_.refs_3_, ...), custom_call_target="tpu_custom_call" | custom-call | flops 167772160 | bytes 1474560 | tf_op jit(solution)/shard_map/down_late/pallas_call | solution.py:269
  119.7 1.7 %collective-permute-done.25.refs_1_ = bf16[640,128]{1,0:T(8,128)(2,1)S(1)} collective-permute-done((bf16[640,128]{1,0:T(8,128)(2,1)S(1)}, bf16[640,128]{1,0:T(8,128)(2,1)S(1)}, u32[]{:S(2)}, u32[]{:S(2)}) %collective-permute-start.25) | collective-permute-done | bytes 163872 | tf_op jit(solution)/shard_map/ppermute | solution.py:53
  123.5 2.9 %collective-permute-start.28 = (bf16[1920,128]{1,0:T(8,128)(2,1)S(1)}, bf16[1920,128]{1,0:T(8,128)(2,1)S(1)}, u32[]{:S(2)}, u32[]{:S(2)}) collective-permute-start(bf16[1920,128]{1,0:T(8,128)(2,1)S(1)} %sum_early.1.own_ref), channel_id=1, source_target_pairs={{0,8},{8,0},{16,24},{24,16},{32,40},{40,32},{48,56},{56,48},{64,72... | collective-permute-start | bytes 1474568 | tf_op jit(solution)/shard_map/ppermute | solution.py:49
  128.2 3.5 %finish_early.1.refs_0_ = bf16[64,5120]{1,0:T(8,128)(2,1)} custom-call(s32[7]{0:T(128)S(1)} %stack.30.place_ref, s32[12]{0:T(128)S(1)} %copy-done.1, bf16[1920,128]{1,0:T(8,128)(2,1)S(1)} %sum_early.1.own_ref, bf16[1920,128]{1,0:T(8,128)(2,1)S(1)} %collective-permute-done.28.got_ref), custom_call_target="tpu_custom_call" | custom-call | flops 62914560 | bytes 1536000 | tf_op jit(solution)/shard_map/finish_early/pallas_call | solution.py:383
  131.8 1.8 %finish_late.1 = bf16[64,5120]{1,0:T(8,128)(2,1)} custom-call(s32[7]{0:T(128)S(1)} %stack.30.place_ref, s32[4]{0:T(128)S(1)} %copy-done, bf16[640,128]{1,0:T(8,128)(2,1)S(1)} %sum_late.1.own_ref, bf16[640,128]{1,0:T(8,128)(2,1)S(1)} %collective-permute-done.27.got_ref, bf16[64,5120]{1,0:T(8,128)(2,1)} %finish_early.1.refs_0_), custom_call_target="tpu_custom_call", output_to_operand_aliasing={{}: (4, {})} | custom-call | flops 20971520 | bytes 512000 | tf_op jit(solution)/shard_map/finish_late/pallas_call | solution.py:383
  (71 shorter events, 28.5 us)
Async XLA Ops:
  0.0 16.7 %copy-start.2 = (bf16[1,512,1024]{2,1,0:T(8,128)(2,1)S(1)}, bf16[1,512,1024]{2,1,0:T(8,128)(2,1)}, u32[]{:S(2)}) copy-start(bf16[1,512,1024]{2,1,0:T(8,128)(2,1)} %param.9) | copy-start | bytes 3145732
  0.0 16.7 %copy-start.3 = (bf16[1,512,128]{2,1,0:T(8,128)(2,1)S(1)}, bf16[1,512,128]{2,1,0:T(8,128)(2,1)}, u32[]{:S(2)}) copy-start(bf16[1,512,128]{2,1,0:T(8,128)(2,1)} %param.10) | copy-start | bytes 393220
  0.0 16.7 %copy-start.4 = (bf16[1,512,128]{2,1,0:T(8,128)(2,1)S(1)}, bf16[1,512,128]{2,1,0:T(8,128)(2,1)}, u32[]{:S(2)}) copy-start(bf16[1,512,128]{2,1,0:T(8,128)(2,1)} %param.11) | copy-start | bytes 393220
  0.0 16.7 %collective-permute-start = (bf16[512,1024]{1,0:T(8,128)(2,1)}, bf16[512,1024]{1,0:T(8,128)(2,1)S(1)}, u32[]{:S(2)}, u32[]{:S(2)}) collective-permute-start(bf16[512,1024]{1,0:T(8,128)(2,1)} %bitcast.107), channel_id=1, source_target_pairs={{0,8},{8,0},{16,24},{24,16},{32,40},{40,32},{48,56},{56,48},{64,72... | collective-permute-start | bytes 3145736 | tf_op jit(solution)/shard_map/ppermute | solution.py:49
  3.2 5.7 %collective-permute-start.1 = (bf16[256,256]{1,0:T(8,128)(2,1)S(1)}, bf16[256,256]{1,0:T(8,128)(2,1)}, u32[]{:S(2)}, u32[]{:S(2)}) collective-permute-start(bf16[256,256]{1,0:T(8,128)(2,1)S(1)} %constant_dynamic-update-slice_fusion), channel_id=1, source_target_pairs={{0,64},{8,72},{16,80},{24,88},{32,96},{40,104},{48,112},{56,120},{... | collective-permute-start | bytes 393224 | tf_op jit(solution)/shard_map/ppermute | solution.py:49
  5.0 8.8 %collective-permute-start.7 = (bf16[256,256]{1,0:T(8,128)(2,1)S(1)}, bf16[256,256]{1,0:T(8,128)(2,1)S(1)}, u32[]{:S(2)}, u32[]{:S(2)}) collective-permute-start(bf16[256,256]{1,0:T(8,128)(2,1)S(1)} %constant_dynamic-update-slice_fusion), channel_id=1, source_target_pairs={{0,8},{8,0},{16,24},{24,16},{32,40},{40,32},{48,56},{56,48},{64,72... | collective-permute-start | bytes 393224 | tf_op jit(solution)/shard_map/ppermute | solution.py:49
  5.5 9.2 %collective-permute-start.5 = (bf16[512,128]{1,0:T(8,128)(2,1)}, bf16[512,128]{1,0:T(8,128)(2,1)S(1)}, u32[]{:S(2)}, u32[]{:S(2)}) collective-permute-start(bf16[512,128]{1,0:T(8,128)(2,1)} %bitcast.112), channel_id=1, source_target_pairs={{0,8},{8,0},{16,24},{24,16},{32,40},{40,32},{48,56},{56,48},{64,72... | collective-permute-start | bytes 393224 | tf_op jit(solution)/shard_map/ppermute | solution.py:49
  5.6 9.9 %collective-permute-start.6 = (bf16[512,128]{1,0:T(8,128)(2,1)}, bf16[512,128]{1,0:T(8,128)(2,1)S(1)}, u32[]{:S(2)}, u32[]{:S(2)}) collective-permute-start(bf16[512,128]{1,0:T(8,128)(2,1)} %bitcast.114), channel_id=1, source_target_pairs={{0,8},{8,0},{16,24},{24,16},{32,40},{40,32},{48,56},{56,48},{64,72... | collective-permute-start | bytes 393224 | tf_op jit(solution)/shard_map/ppermute | solution.py:49
  9.9 13.4 %collective-permute-start.4 = (bf16[2,256,256]{2,1,0:T(8,128)(2,1)S(1)}, bf16[2,256,256]{2,1,0:T(8,128)(2,1)S(1)}, u32[]{:S(2)}, u32[]{:S(2)}) collective-permute-start(bf16[2,256,256]{2,1,0:T(8,128)(2,1)S(1)} %pad_maximum_fusion.1), channel_id=1, source_target_pairs={{0,32},{8,40},{16,48},{24,56},{32,0},{40,8},{48,16},{56,24},{64,96... | collective-permute-start | bytes 786440 | tf_op jit(solution)/shard_map/ppermute | solution.py:49
  13.9 10.6 %collective-permute-start.3 = (bf16[2,256,256]{2,1,0:T(8,128)(2,1)S(1)}, bf16[2,256,256]{2,1,0:T(8,128)(2,1)S(1)}, u32[]{:S(2)}, u32[]{:S(2)}) collective-permute-start(bf16[2,256,256]{2,1,0:T(8,128)(2,1)S(1)} %pad_maximum_fusion.1), channel_id=1, source_target_pairs={{0,48},{8,56},{16,0},{24,8},{32,16},{40,24},{48,32},{56,40},{64,11... | collective-permute-start | bytes 786440 | tf_op jit(solution)/shard_map/ppermute | solution.py:49
  14.7 9.8 %collective-permute-start.2 = (bf16[2,256,256]{2,1,0:T(8,128)(2,1)S(1)}, bf16[2,256,256]{2,1,0:T(8,128)(2,1)S(1)}, u32[]{:S(2)}, u32[]{:S(2)}) collective-permute-start(bf16[2,256,256]{2,1,0:T(8,128)(2,1)S(1)} %pad_maximum_fusion.1), channel_id=1, source_target_pairs={{0,16},{8,24},{16,32},{24,40},{32,48},{40,56},{48,0},{56,8},{64,80... | collective-permute-start | bytes 786440 | tf_op jit(solution)/shard_map/ppermute | solution.py:49
  15.4 14.6 %collective-permute-start.8 = (bf16[320,1024]{1,0:T(8,128)(2,1)S(1)}, bf16[320,1024]{1,0:T(8,128)(2,1)S(1)}, u32[]{:S(2)}, u32[]{:S(2)}) collective-permute-start(bf16[320,1024]{1,0:T(8,128)(2,1)S(1)} %bitcast.118), channel_id=1, source_target_pairs={{0,64},{8,72},{16,80},{24,88},{32,96},{40,104},{48,112},{56,120},{... | collective-permute-start | bytes 1966088 | tf_op jit(solution)/shard_map/ppermute | solution.py:49
  30.1 28.5 %collective-permute-start.11 = (bf16[640,1024]{1,0:T(8,128)(2,1)S(1)}, bf16[640,1024]{1,0:T(8,128)(2,1)S(1)}, u32[]{:S(2)}, u32[]{:S(2)}) collective-permute-start(bf16[640,1024]{1,0:T(8,128)(2,1)S(1)} %constant_dynamic-update-slice_fusion.2.refs_0_.refs_1_.refs_2_.refs_3_), channel_id=1, source_target_pairs={{0,48},{8,56},{16,0},{24,8},{32,16},{40,24},{48,32},{56,40},{64,11... | collective-permute-start | bytes 3932168 | tf_op jit(solution)/shard_map/ppermute | solution.py:49
  32.1 28.7 %collective-permute-start.10 = (bf16[640,1024]{1,0:T(8,128)(2,1)S(1)}, bf16[640,1024]{1,0:T(8,128)(2,1)S(1)}, u32[]{:S(2)}, u32[]{:S(2)}) collective-permute-start(bf16[640,1024]{1,0:T(8,128)(2,1)S(1)} %constant_dynamic-update-slice_fusion.2.refs_0_.refs_1_.refs_2_.refs_3_), channel_id=1, source_target_pairs={{0,16},{8,24},{16,32},{24,40},{32,48},{40,56},{48,0},{56,8},{64,80... | collective-permute-start | bytes 3932168 | tf_op jit(solution)/shard_map/ppermute | solution.py:49
  33.2 13.9 %collective-permute-start.9 = (bf16[7,256,256]{2,1,0:T(8,128)(2,1)S(1)}, bf16[7,256,256]{2,1,0:T(8,128)(2,1)S(1)}, u32[]{:S(2)}, u32[]{:S(2)}) collective-permute-start(bf16[7,256,256]{2,1,0:T(8,128)(2,1)S(1)} %pad_maximum_fusion.refs_0_), channel_id=1, source_target_pairs={{0,8},{8,0},{16,24},{24,16},{32,40},{40,32},{48,56},{56,48},{64,72... | collective-permute-start | bytes 2752520 | tf_op jit(solution)/shard_map/ppermute | solution.py:49
  57.5 9.6 %collective-permute-start.14 = (bf16[1,512,512]{2,1,0:T(8,128)(2,1)S(1)}, bf16[1,512,512]{2,1,0:T(8,128)(2,1)S(1)}, u32[]{:S(2)}, u32[]{:S(2)}) collective-permute-start(bf16[1,512,512]{2,1,0:T(8,128)(2,1)S(1)} %attend_partner.1), channel_id=1, source_target_pairs={{0,8},{8,0},{16,24},{24,16},{32,40},{40,32},{48,56},{56,48},{64,72... | collective-permute-start | bytes 1572872 | tf_op jit(solution)/shard_map/ppermute | solution.py:49
  58.5 8.6 %collective-permute-start.15 = (bf16[1,512,512]{2,1,0:T(8,128)(2,1)S(1)}, bf16[1,512,512]{2,1,0:T(8,128)(2,1)S(1)}, u32[]{:S(2)}, u32[]{:S(2)}) collective-permute-start(bf16[1,512,512]{2,1,0:T(8,128)(2,1)S(1)} %attend_own.1), channel_id=1, source_target_pairs={{0,8},{8,0},{16,24},{24,16},{32,40},{40,32},{48,56},{56,48},{64,72... | collective-permute-start | bytes 1572872 | tf_op jit(solution)/shard_map/ppermute | solution.py:49
  60.9 20.6 %collective-permute-start.12 = (bf16[320,1024]{1,0:T(8,128)(2,1)S(1)}, bf16[320,1024]{1,0:T(8,128)(2,1)S(1)}, u32[]{:S(2)}, u32[]{:S(2)}) collective-permute-start(bf16[320,1024]{1,0:T(8,128)(2,1)S(1)} %slice.6), channel_id=1, source_target_pairs={{0,16},{8,24},{16,32},{24,40},{32,48},{40,56},{48,0},{56,8},{64,80... | collective-permute-start | bytes 1966088 | tf_op jit(solution)/shard_map/ppermute | solution.py:49
  61.0 22.9 %collective-permute-start.13 = (bf16[320,1024]{1,0:T(8,128)(2,1)S(1)}, bf16[320,1024]{1,0:T(8,128)(2,1)S(1)}, u32[]{:S(2)}, u32[]{:S(2)}) collective-permute-start(bf16[320,1024]{1,0:T(8,128)(2,1)S(1)} %slice.7), channel_id=1, source_target_pairs={{0,48},{8,56},{16,0},{24,8},{32,16},{40,24},{48,32},{56,40},{64,11... | collective-permute-start | bytes 1966088 | tf_op jit(solution)/shard_map/ppermute | solution.py:49
  71.5 14.5 %collective-permute-start.16 = (bf16[960,256]{1,0:T(8,128)(2,1)S(1)}, bf16[960,256]{1,0:T(8,128)(2,1)S(1)}, u32[]{:S(2)}, u32[]{:S(2)}) collective-permute-start(bf16[960,256]{1,0:T(8,128)(2,1)S(1)} %far_top_early.1), channel_id=1, source_target_pairs={{0,2},{1,3},{2,4},{3,5},{4,6},{5,7},{6,0},{7,1},{8,10},{9,11},{10,... | collective-permute-start | bytes 1474568 | tf_op jit(solution)/shard_map/ppermute | solution.py:53
  72.8 13.2 %collective-permute-start.17 = (bf16[960,256]{1,0:T(8,128)(2,1)S(1)}, bf16[960,256]{1,0:T(8,128)(2,1)S(1)}, u32[]{:S(2)}, u32[]{:S(2)}) collective-permute-start(bf16[960,256]{1,0:T(8,128)(2,1)S(1)} %far_low_early.1), channel_id=1, source_target_pairs={{0,6},{1,7},{2,0},{3,1},{4,2},{5,3},{6,4},{7,5},{8,14},{9,15},{10,... | collective-permute-start | bytes 1474568 | tf_op jit(solution)/shard_map/ppermute | solution.py:53
  76.6 23.1 %collective-permute-start.20 = (bf16[960,256]{1,0:T(8,128)(2,1)S(1)}, bf16[960,256]{1,0:T(8,128)(2,1)S(1)}, u32[]{:S(2)}, u32[]{:S(2)}) collective-permute-start(bf16[960,256]{1,0:T(8,128)(2,1)S(1)} %up_low_early.1), channel_id=1, source_target_pairs={{0,2},{1,3},{2,4},{3,5},{4,6},{5,7},{6,0},{7,1},{8,10},{9,11},{10,... | collective-permute-start | bytes 1474568 | tf_op jit(solution)/shard_map/ppermute | solution.py:53
  81.4 18.2 %collective-permute-start.21 = (bf16[960,256]{1,0:T(8,128)(2,1)S(1)}, bf16[960,256]{1,0:T(8,128)(2,1)S(1)}, u32[]{:S(2)}, u32[]{:S(2)}) collective-permute-start(bf16[960,256]{1,0:T(8,128)(2,1)S(1)} %down_top_early.1), channel_id=1, source_target_pairs={{0,6},{1,7},{2,0},{3,1},{4,2},{5,3},{6,4},{7,5},{8,14},{9,15},{10,... | collective-permute-start | bytes 1474568 | tf_op jit(solution)/shard_map/ppermute | solution.py:53
  90.5 15.1 %collective-permute-start.22 = (bf16[960,256]{1,0:T(8,128)(2,1)S(1)}, bf16[960,256]{1,0:T(8,128)(2,1)S(1)}, u32[]{:S(2)}, u32[]{:S(2)}) collective-permute-start(bf16[960,256]{1,0:T(8,128)(2,1)S(1)} %down_low_early.1), channel_id=1, source_target_pairs={{0,6},{1,7},{2,0},{3,1},{4,2},{5,3},{6,4},{7,5},{8,14},{9,15},{10,... | collective-permute-start | bytes 1474568 | tf_op jit(solution)/shard_map/ppermute | solution.py:53
  91.7 13.8 %collective-permute-start.19 = (bf16[960,256]{1,0:T(8,128)(2,1)S(1)}, bf16[960,256]{1,0:T(8,128)(2,1)S(1)}, u32[]{:S(2)}, u32[]{:S(2)}) collective-permute-start(bf16[960,256]{1,0:T(8,128)(2,1)S(1)} %up_top_early.1), channel_id=1, source_target_pairs={{0,2},{1,3},{2,4},{3,5},{4,6},{5,7},{6,0},{7,1},{8,10},{9,11},{10,... | collective-permute-start | bytes 1474568 | tf_op jit(solution)/shard_map/ppermute | solution.py:53
  92.0 17.5 %collective-permute-start.18 = (bf16[640,512]{1,0:T(8,128)(2,1)S(1)}, bf16[640,512]{1,0:T(8,128)(2,1)S(1)}, u32[]{:S(2)}, u32[]{:S(2)}) collective-permute-start(bf16[640,512]{1,0:T(8,128)(2,1)S(1)} %give_late.1), channel_id=1, source_target_pairs={{0,1},{1,0},{2,3},{3,2},{4,5},{5,4},{6,7},{7,6},{8,9},{9,8},{10,11... | collective-permute-start | bytes 1966088 | tf_op jit(solution)/shard_map/ppermute | solution.py:53
  106.0 17.0 %collective-permute-start.23 = (bf16[1920,128]{1,0:T(8,128)(2,1)S(1)}, bf16[1920,128]{1,0:T(8,128)(2,1)S(1)}, u32[]{:S(2)}, u32[]{:S(2)}) collective-permute-start(bf16[1920,128]{1,0:T(8,128)(2,1)S(1)} %give_early.1), channel_id=1, source_target_pairs={{0,1},{1,0},{2,3},{3,2},{4,5},{5,4},{6,7},{7,6},{8,9},{9,8},{10,11... | collective-permute-start | bytes 1474568 | tf_op jit(solution)/shard_map/ppermute | solution.py:53
  111.1 8.6 %collective-permute-start.24 = (bf16[640,128]{1,0:T(8,128)(2,1)S(1)}, bf16[640,128]{1,0:T(8,128)(2,1)S(1)}, u32[]{:S(2)}, u32[]{:S(2)}) collective-permute-start(bf16[640,128]{1,0:T(8,128)(2,1)S(1)} %far_late.1), channel_id=1, source_target_pairs={{0,4},{1,5},{2,6},{3,7},{4,0},{5,1},{6,2},{7,3},{8,12},{9,13},{10,... | collective-permute-start | bytes 491528 | tf_op jit(solution)/shard_map/ppermute | solution.py:53
  115.2 6.2 %collective-permute-start.25 = (bf16[640,128]{1,0:T(8,128)(2,1)S(1)}, bf16[640,128]{1,0:T(8,128)(2,1)S(1)}, u32[]{:S(2)}, u32[]{:S(2)}) collective-permute-start(bf16[640,128]{1,0:T(8,128)(2,1)S(1)} %up_late.1), channel_id=1, source_target_pairs={{0,2},{1,3},{2,4},{3,5},{4,6},{5,7},{6,0},{7,1},{8,10},{9,11},{10,... | collective-permute-start | bytes 491528 | tf_op jit(solution)/shard_map/ppermute | solution.py:53
  118.4 4.5 %collective-permute-start.26 = (bf16[640,128]{1,0:T(8,128)(2,1)S(1)}, bf16[640,128]{1,0:T(8,128)(2,1)S(1)}, u32[]{:S(2)}, u32[]{:S(2)}) collective-permute-start(bf16[640,128]{1,0:T(8,128)(2,1)S(1)} %down_late.1), channel_id=1, source_target_pairs={{0,6},{1,7},{2,0},{3,1},{4,2},{5,3},{6,4},{7,5},{8,14},{9,15},{10,... | collective-permute-start | bytes 491528 | tf_op jit(solution)/shard_map/ppermute | solution.py:53
  123.5 4.7 %collective-permute-start.28 = (bf16[1920,128]{1,0:T(8,128)(2,1)S(1)}, bf16[1920,128]{1,0:T(8,128)(2,1)S(1)}, u32[]{:S(2)}, u32[]{:S(2)}) collective-permute-start(bf16[1920,128]{1,0:T(8,128)(2,1)S(1)} %sum_early.1.own_ref), channel_id=1, source_target_pairs={{0,8},{8,0},{16,24},{24,16},{32,40},{40,32},{48,56},{56,48},{64,72... | collective-permute-start | bytes 1474568 | tf_op jit(solution)/shard_map/ppermute | solution.py:49
  128.1 3.7 %collective-permute-start.27 = (bf16[640,128]{1,0:T(8,128)(2,1)S(1)}, bf16[640,128]{1,0:T(8,128)(2,1)S(1)}, u32[]{:S(2)}, u32[]{:S(2)}) collective-permute-start(bf16[640,128]{1,0:T(8,128)(2,1)S(1)} %sum_late.1.own_ref), channel_id=1, source_target_pairs={{0,8},{8,0},{16,24},{24,16},{32,40},{40,32},{48,56},{56,48},{64,72... | collective-permute-start | bytes 491528 | tf_op jit(solution)/shard_map/ppermute | solution.py:49
  (4 other events, 25.3 us)
